TPU v7x, 256 devices: a whole 4x4x8 slice. The times are simulated.
256 devices in a mesh: dp: 16 (over x_lo, y, core), mp: 16 (over z, x_hi).
Axes of the slice: x: 4 (x_hi: 2, x_lo: 2; x = x_hi * 2 + x_lo), y: 4, z: 8, core: 2. Of those that a mesh axis runs over, the one named last changes fastest.
Arguments:
- image_feats: bfloat16 [8192, 1152], P('dp'), may hold values from -10 to 10
- text_feats: bfloat16 [8192, 1152], P(('dp', 'mp')), may hold values from -10 to 10
- w_in: bfloat16 [1152, 4096], P(None, 'mp'), may hold values from -0.1875 to 0.1875
- w_out: bfloat16 [4096, 1152], P('mp'), may hold values from -0.09375 to 0.09375
- image_bucket: int32 [8192], P('dp'), may hold values from 0 to 7
- text_bucket: int32 [8192], P(('dp', 'mp')), may hold values from 0 to 7
- positive: int32 [8192], P('dp'), may hold values from 0 to 8191, each once
- reward_table: float32 [8, 8], replicated, may hold values from 0.05 to 80
Outputs:
- pair_loss: float32 [], replicated
- grad_text: float32 [8192, 1152], P(('dp', 'mp'))
- grad_image: float32 [8192, 1152], P(('dp', 'mp'))
- grad_w_in: float32 [1152, 4096], P(None, 'mp')
- grad_w_out: float32 [4096, 1152], P('mp')
Inputs may be any that keep to these rules, and one draw needn't show every extreme that they name: `positive`: every caption is the match of exactly one image.
All inputs are finite; a program needn't handle non-finite values.
Results may differ from a plain program's by a relative error of at most 0.0029.
Values may be sent and summed in bfloat16 or wider, within the bound.
A program may use at most 64 MiB of HBM per device.

v0:
```python
import jax
import jax.numpy as jnp
from jax import lax
from jax.sharding import PartitionSpec as P

logit_scale = 4.0
logit_bias = -2.0
norm_eps = 1e-06
root_coef = 0.7978845608028654
cubic_coef = 0.044715


def from_behind(value, axis, steps):
    count = lax.axis_size(axis)
    pairs = [(source, (source + steps) % count) for source in range(count)]
    return lax.ppermute(value, axis, pairs)


def gelu_tanh(values):
    return (
        0.5
        * values
        * (1.0 + jnp.tanh(root_coef * (values + cubic_coef * values * values * values)))
    )


def gelu_slope(values):
    tangent = jnp.tanh(root_coef * (values + cubic_coef * values * values * values))
    return 0.5 * (1.0 + tangent) + 0.5 * values * (1.0 - tangent * tangent) * root_coef * (
        1.0 + 3.0 * cubic_coef * values * values
    )


def row_norm(values):
    return jnp.sqrt(jnp.sum(values * values, axis=-1, keepdims=True) + norm_eps)


def pair_block(text_rows, hot_rows, text_index, image_emb, image_weight, positive):
    logits = (
        logit_scale
        * lax.dot_general(
            text_rows, image_emb, (((1,), (1,)), ((), ())), preferred_element_type=jnp.float32
        )
        + logit_bias
    )
    signed = jnp.where(text_index[:, None] == positive[None, :], 1.0, -1.0)
    weight = jnp.dot(hot_rows.astype(jnp.float32), image_weight.T, precision=lax.Precision.HIGHEST)
    margin = signed * logits
    loss_sum = jnp.sum(weight * jax.nn.softplus(-margin))
    coefficient = (-logit_scale * weight * signed * jax.nn.sigmoid(-margin)).astype(jnp.bfloat16)
    return (loss_sum, coefficient)


def per_device(
    image_feats, text_feats, w_in, w_out, image_bucket, text_bucket, positive, reward_table
):
    loop_size = lax.axis_size("dp")
    model_size = lax.axis_size("mp")
    data_index = lax.axis_index("dp")
    model_index = lax.axis_index("mp")
    group_rows = image_feats.shape[0]
    own_rows = text_feats.shape[0]
    levels = reward_table.shape[0]
    own_start = model_index * own_rows
    hidden_pre = jnp.dot(image_feats, w_in, preferred_element_type=jnp.float32)
    activation = gelu_tanh(hidden_pre).astype(jnp.bfloat16)
    branch_own = lax.psum_scatter(
        jnp.dot(activation, w_out, preferred_element_type=jnp.float32),
        "mp",
        scatter_dimension=0,
        tiled=True,
    )
    features_own = (
        lax.dynamic_slice_in_dim(image_feats, own_start, own_rows, 0).astype(jnp.float32)
        + branch_own
    )
    norm_own = row_norm(features_own)
    unit_own = features_own / norm_own
    image_emb = lax.all_gather(unit_own.astype(jnp.bfloat16), "mp", axis=0, tiled=True)
    text_wide = text_feats.astype(jnp.float32)
    text_emb = (text_wide / row_norm(text_wide)).astype(jnp.bfloat16)
    levels_row = jnp.arange(levels, dtype=jnp.int32)
    text_hot = (text_bucket[:, None] == levels_row[None, :]).astype(jnp.bfloat16)
    image_hot = (image_bucket[:, None] == levels_row[None, :]).astype(jnp.float32)
    image_weight = jnp.dot(image_hot, reward_table, precision=lax.Precision.HIGHEST)
    within = jnp.arange(own_rows, dtype=jnp.int32)

    def turn(turn_index, state_now):
        text_block, hot_block, carried, image_grad, loss_sum = state_now
        anchor = (data_index - turn_index) % loop_size
        text_index = (anchor * model_size + model_index) * own_rows + within
        block_loss, coefficient = pair_block(
            text_block, hot_block, text_index, image_emb, image_weight, positive
        )
        image_grad = image_grad + lax.dot_general(
            coefficient, text_block, (((0,), (0,)), ((), ())), preferred_element_type=jnp.float32
        )
        carried = carried + jnp.dot(coefficient, image_emb, preferred_element_type=jnp.float32)
        text_block, hot_block = from_behind((text_block, hot_block), "dp", 1)
        carried = from_behind(carried, "dp", 1)
        return (text_block, hot_block, carried, image_grad, loss_sum + block_loss)

    start_state = (
        text_emb,
        text_hot,
        jnp.zeros(text_emb.shape, jnp.float32),
        jnp.zeros(image_emb.shape, jnp.float32),
        jnp.zeros((), jnp.float32),
    )
    final_state = lax.fori_loop(0, loop_size, turn, start_state)
    grad_text = final_state[2]
    image_grad = final_state[3]
    loss_sum = final_state[4]
    pair_count = float(group_rows * loop_size)
    pair_loss = lax.psum(loss_sum, ("dp", "mp")) / (pair_count * pair_count)
    own_grad = lax.psum_scatter(image_grad, "mp", scatter_dimension=0, tiled=True)
    projected = jnp.sum(unit_own * own_grad, axis=-1, keepdims=True)
    grad_features = (own_grad - unit_own * projected) / norm_own
    grad_feat_b = grad_features.astype(jnp.bfloat16)
    grad_feat_all = lax.all_gather(grad_feat_b, "mp", axis=0, tiled=True)
    grad_act = lax.dot_general(
        grad_feat_all, w_out, (((1,), (1,)), ((), ())), preferred_element_type=jnp.float32
    )
    grad_hidden = (grad_act * gelu_slope(hidden_pre)).astype(jnp.bfloat16)
    grad_image = grad_features + lax.psum_scatter(
        lax.dot_general(
            grad_hidden, w_in, (((1,), (1,)), ((), ())), preferred_element_type=jnp.float32
        ),
        "mp",
        scatter_dimension=0,
        tiled=True,
    )
    local_w_in = lax.dot_general(
        image_feats, grad_hidden, (((0,), (0,)), ((), ())), preferred_element_type=jnp.float32
    )
    local_w_out = lax.dot_general(
        activation, grad_feat_all, (((0,), (0,)), ((), ())), preferred_element_type=jnp.float32
    )
    grad_w_in, grad_w_out = lax.psum((local_w_in, local_w_out), "dp")
    return (pair_loss, grad_text, grad_image, grad_w_in, grad_w_out)


def solution(mesh):
    return jax.shard_map(
        per_device,
        mesh=mesh,
        in_specs=(
            P("dp", None),
            P(("dp", "mp"), None),
            P(None, "mp"),
            P("mp", None),
            P("dp"),
            P(("dp", "mp")),
            P("dp"),
            P(),
        ),
        out_specs=(P(), P(("dp", "mp"), None), P(("dp", "mp"), None), P(None, "mp"), P("mp", None)),
        check_vma=False,
    )
```

profile of v0, /device:TPU:1, one launch (start us, length us, event | category | flops | bytes accessed | tf_op | source)
XLA Modules:
  0.0 1113.1 jit_solution(11979203233872048087)
XLA Ops:
  12.1 211.0 %reduce-scatter.4.cloned.1.call-done = f32[32,1152]{1,0:T(8,128)} async-done(((f32[512,1152]{1,0:T(8,128)}), f32[32,1152]{1,0:T(8,128)}) %reduce-scatter.4.cloned.1.call-update) | async-done | bytes 147472 | tf_op jit(solution)/shard_map/reduce_scatter | solution.py:67
  226.5 78.1 %all-gather.3.cloned.1.call-done = bf16[512,1152]{1,0:T(8,128)(2,1)} async-done(((bf16[32,1152]{1,0:T(8,128)(2,1)}), bf16[512,1152]{1,0:T(8,128)(2,1)}) %all-gather.3.cloned.1.call-update) | async-done | bytes 1179664 | tf_op jit(solution)/shard_map/all_gather | solution.py:79
  304.6 162.7 %while.24 = (s32[]{:T(128)}, bf16[32,1152]{1,0:T(8,128)(2,1)S(1)}, bf16[32,8]{0,1:T(8,128)(2,1)S(1)}, f32[32,1152]{1,0:T(8,128)S(1)}, f32[512,1152]{1,0:T(8,128)...) while((s32[]{:T(128)}, bf16[32,1152]{1,0:T(8,128)(2,1)S(1)}, ...), condition=%wide.region_5.6_spmd.clone, body=%wide.region_3.5_spmd.clone.sunk | while | flops 116396080 | bytes 13525348 | solution.py:110
  304.7 5.6 collective-permute-start.1
  323.7 3.6 convolution_add_fusion.5
  331.8 3.6 convolution_add_fusion.5
  336.1 3.6 collective-permute-start.1
  343.1 3.6 convolution_add_fusion.5
  352.9 3.6 convolution_add_fusion.5
  357.2 2.2 collective-permute-start.1
  363.4 3.6 convolution_add_fusion.5
  367.6 2.4 collective-permute-start.1
  373.4 3.6 convolution_add_fusion.5
  377.7 2.3 collective-permute-start.1
  383.4 3.6 convolution_add_fusion.5
  393.2 3.6 convolution_add_fusion.5
  403.1 3.6 convolution_add_fusion.5
  413.0 3.6 convolution_add_fusion.5
  423.2 3.6 convolution_add_fusion.5
  427.4 2.4 collective-permute-start.1
  433.2 3.6 convolution_add_fusion.5
  437.5 2.3 collective-permute-start.1
  443.2 3.6 convolution_add_fusion.5
  447.5 2.3 collective-permute-start.1
  453.2 3.6 convolution_add_fusion.5
  463.1 3.6 convolution_add_fusion.5
  467.4 206.0 %reduce-scatter.6.cloned.1.call-done = f32[32,1152]{1,0:T(8,128)} async-done(((f32[512,1152]{1,0:T(8,128)}), f32[32,1152]{1,0:T(8,128)}) %reduce-scatter.6.cloned.1.call-update) | async-done | bytes 147472 | tf_op jit(solution)/shard_map/reduce_scatter | solution.py:116
  676.2 78.1 %all-gather.5.cloned.1.call-done = bf16[512,1152]{1,0:T(8,128)(2,1)} async-done(((bf16[32,1152]{1,0:T(8,128)(2,1)}), bf16[512,1152]{1,0:T(8,128)(2,1)}) %all-gather.5.cloned.1.call-update) | async-done | bytes 1179664 | tf_op jit(solution)/shard_map/all_gather | solution.py:120
  762.5 79.3 %psum.21 = f32[]{:T(128)} all-reduce(f32[]{:T(128)} %get-tuple-element.294), channel_id=1, replica_groups=mesh['dp'=16,'mp'=16] {'dp','mp'}, use_global_device_ids=true, to_apply=%region_6.7 | all-reduce | flops 1 | bytes 8 | tf_op jit(solution)/shard_map/psum | solution.py:115
  842.5 46.6 %all-reduce.3.cloned.1.call-done = (f32[1152,256]{0,1:T(8,128)}, f32[256,1152]{1,0:T(8,128)}) async-done(((f32[1152,256]{0,1:T(8,128)}, f32[256,1152]{1,0:T(8,128)}), (f32[1152,256]{0,1:T(8,128)}, f32[256,1152]{1,0:T(8,128)})) %all-reduce.3.cloned.1.call-update) | async-done | bytes 2359312 | tf_op jit(solution)/shard_map/psum | solution.py:139
  889.1 2.8 copy.13
  891.9 209.9 %reduce-scatter.8.cloned.1.call-done = f32[32,1152]{1,0:T(8,128)} async-done(((f32[512,1152]{1,0:T(8,128)}), f32[32,1152]{1,0:T(8,128)}) %reduce-scatter.8.cloned.1.call-update) | async-done | bytes 147472 | tf_op jit(solution)/shard_map/reduce_scatter | solution.py:125
  (278 shorter events, 97.2 us)
Async XLA Ops:
  7.2 215.9 %reduce-scatter.4.cloned.1.call-start = ((), (), s32[]{:S(2)}) async-start(), calls=%async_computation.3 | async-start | bytes 2506752 | tf_op jit(solution)/shard_map/reduce_scatter | solution.py:67
  12.1 292.5 %all-gather.3.cloned.1.call-start = ((), (), s32[]{:S(2)}) async-start(), calls=%async_computation.4 | async-start | bytes 1253376 | tf_op jit(solution)/shard_map/all_gather | solution.py:79
  225.8 447.6 %reduce-scatter.6.cloned.1.call-start = ((), (), s32[]{:S(2)}) async-start(), calls=%async_computation.5 | async-start | bytes 2506752 | tf_op jit(solution)/shard_map/reduce_scatter | solution.py:116
  304.7 12.7 %collective-permute-start.1 = (bf16[32,8]{0,1:T(8,128)(2,1)S(1)}, bf16[32,8]{0,1:T(8,128)(2,1)S(1)}, u32[]{:S(2)}, u32[]{:S(2)}) collective-permute-start(bf16[32,8]{0,1:T(8,128)(2,1)S(1)} %copy.22), channel_id=1, source_target_pairs={{0,16},{16,32},{32,48},{48,64},{64,80},{80,96},{96,112},{112,128},... | collective-permute-start | bytes 1544 | tf_op jit(solution)/shard_map/while/body/eval_jaxpr/ppermute | solution.py:16
  317.4 10.4 collective-permute-start.1
  319.4 8.5 collective-permute-start
  328.0 8.1 collective-permute-start.1
  328.2 7.8 collective-permute-start
  336.1 11.2 %collective-permute-start.1 = (bf16[32,8]{0,1:T(8,128)(2,1)S(1)}, bf16[32,8]{0,1:T(8,128)(2,1)S(1)}, u32[]{:S(2)}, u32[]{:S(2)}) collective-permute-start(bf16[32,8]{0,1:T(8,128)(2,1)S(1)} %copy.22), channel_id=1, source_target_pairs={{0,16},{16,32},{32,48},{48,64},{64,80},{80,96},{96,112},{112,128},... | collective-permute-start | bytes 1544 | tf_op jit(solution)/shard_map/while/body/eval_jaxpr/ppermute | solution.py:16
  339.7 7.6 collective-permute-start
  347.4 9.8 collective-permute-start.1
  357.2 10.4 collective-permute-start.1
  359.4 8.2 collective-permute-start
  367.6 10.0 collective-permute-start.1
  377.7 9.9 collective-permute-start.1
  380.0 7.6 collective-permute-start
  387.7 9.8 collective-permute-start.1
  397.5 9.8 collective-permute-start.1
  399.7 7.6 collective-permute-start
  407.4 9.8 collective-permute-start.1
  417.2 10.1 collective-permute-start.1
  419.4 8.0 collective-permute-start
  427.4 10.0 collective-permute-start.1
  429.8 7.6 collective-permute-start
  437.5 9.9 collective-permute-start.1
  439.8 7.6 collective-permute-start
  447.5 9.9 collective-permute-start.1
  449.8 7.6 collective-permute-start
  457.5 9.8 collective-permute-start.1
  467.4 287.0 %all-gather.5.cloned.1.call-start = ((), (), s32[]{:S(2)}) async-start(), calls=%async_computation.6 | async-start | bytes 1253376 | tf_op jit(solution)/shard_map/all_gather | solution.py:120
  676.2 213.0 %all-reduce.3.cloned.1.call-start = ((), (), s32[]{:S(2)}) async-start(), calls=%async_computation.8 | async-start | bytes 4718592 | tf_op jit(solution)/shard_map/psum | solution.py:139
  759.5 342.3 %reduce-scatter.8.cloned.1.call-start = ((), (), s32[]{:S(2)}) async-start(), calls=%async_computation.7 | async-start | bytes 2506752 | tf_op jit(solution)/shard_map/reduce_scatter | solution.py:125
  (52 other events, 2489.0 us)
Sparse Core Ops, SparseCore 0:
  12.2 210.8 reduce-scatter.3
  226.2 78.3 all-gather.2
  467.5 205.8 reduce-scatter.5
  676.4 77.8 all-gather.4
  759.6 129.4 all-reduce.2
  892.9 208.7 reduce-scatter.7
where the time goes:
time: 1120 us; the launch traced here: 1110 us
  waiting for transfers between devices  830 us (74%)
  matrix products  113 us (10%)
  blocking collectives  79.3 us (7%)
  starting transfers between devices  49.6 us (4%)
  between operations  16.1 us (1%)
  loops' own time  11.5 us (1%)
    reduce_scatter x1, waiting for transfers between devices, per_device(): lax.psum_scatter(jnp.dot(activation, w_out, preferred_element_type=jnp.fl...  211 us
    reduce_scatter x1, waiting for transfers between devices, per_device(): lax.psum_scatter(lax.dot_general(grad_hidden, w_in, (((1,), (1,)), ((), (...  210 us
    reduce_scatter x1, waiting for transfers between devices, per_device(): lax.psum_scatter(image_grad, 'mp', scatter_dimension=0, tiled=True)  206 us
    psum x1, blocking collectives, per_device(): pair_loss = lax.psum(loss_sum, ('dp', 'mp')) / (pair_count * pair_count)  79.3 us
    all_gather x1, waiting for transfers between devices, per_device(): lax.all_gather(unit_own.astype(jnp.bfloat16), 'mp', axis=0, tiled=True)  78.1 us
    all_gather x1, waiting for transfers between devices, per_device(): grad_feat_all = lax.all_gather(grad_feat_b, 'mp', axis=0, tiled=True)  78.1 us
    dot_general x16, matrix products, turn(): lax.dot_general(coefficient, text_block, (((0,), (0,)), ((), ())), prefer...  55.5 us
    ppermute x48, starting transfers between devices, from_behind(): return lax.ppermute(value, axis, pairs)  49.3 us
  transfers between devices with their start and end apart: 54, of which 6 were waited for; matrix products, arithmetic and copies ran while one was open for 10% of the time, Pallas kernels for 0%

commit v1 on v0

v1 whole, which is shorter than its diff:
```python
import jax
import jax.numpy as jnp
from jax import lax
from jax.experimental import pallas as pl
from jax.experimental.pallas import tpu as pltpu
from jax.sharding import PartitionSpec as P

MESH = pl.DeviceIdType.MESH
F32 = jnp.float32
BF16 = jnp.bfloat16

logit_scale = 4.0
logit_bias = -2.0
norm_eps = 1e-06
root_coef = 0.7978845608028654
cubic_coef = 0.044715

D = 1152
ROWS = 512
OWN = 32
HID = 256
PAIRS = 8192.0 * 8192.0
ext = 128
VMEM_LIMIT = 50 * 2**20

NT = (((1,), (1,)), ((), ()))
TN = (((0,), (0,)), ((), ()))


def dot(a, b):
    return jnp.dot(a, b, preferred_element_type=F32)


def dot_nt(a, b):
    return lax.dot_general(a, b, NT, preferred_element_type=F32)


def dot_tn(a, b):
    return lax.dot_general(a, b, TN, preferred_element_type=F32)


def gelu_tanh(v):
    return 0.5 * v * (1.0 + jnp.tanh(root_coef * (v + cubic_coef * v * v * v)))


def gelu_slope(v):
    t = jnp.tanh(root_coef * (v + cubic_coef * v * v * v))
    return 0.5 * (1.0 + t) + 0.5 * v * (1.0 - t * t) * root_coef * (1.0 + 3.0 * cubic_coef * v * v)


def row_norm(v):
    return jnp.sqrt(jnp.sum(v * v, axis=-1, keepdims=True) + norm_eps)


(TEXT, META, RS1, AG1C, RS2C, RS2Z, TG, LOSS1, LOSSC, LOSSZ, AG2, RS3, ARC_I, ARC_O, ARS_I, ARS_O, AAG_I, AAG_O,
 AFC_I, AFC_O, AG1Z) = range(21)


def rows_at(start, count, step):
    return pl.ds(pl.multiple_of(start, step), count)


def kernel(
    x_ref, t_ref, wi_ref, wo_ref, ib_ref, tb_ref, pos_ref, tab_ref,
    loss_ref, gt_ref, gi_ref, gwi_ref, gwo_ref,
    hp, act, rs1s, rs1r, txt, meta, hot, img, coef, loss_acc, c_send, c_recv, ig, rs2s, rs2r, tgs, tgr,
    l_tile, l1r, lc_tile, lcr, lz_tile, lzr, gfall, gh, rs3s, rs3r,
    arc_si, arc_so, arc_ri, arc_ro, awi, awo, ars_si, ars_so, ars_ri, ars_ro, fwi, fwo,
    ssem, rsem, zsem,
):
    dp, mp = lax.axis_index("dp"), lax.axis_index("mp")
    core, y, xl = lax.rem(dp, 2), lax.rem(dp // 2, 4), dp // 8
    xh, z = lax.rem(mp, 2), mp // 2
    x = xh * 2 + xl
    partner = (dp + 1 - 2 * core, mp)

    def mp_peer(j):
        return (dp, lax.rem(mp + j, 16))

    def z_peer(j):
        return (dp, lax.rem(z + j, 8) * 2 + xh)

    def plane_dev(x2, y2):
        return ((lax.rem(x2, 2) * 4 + y2) * 2 + core, z * 2 + x2 // 2)

    def ar_peer(j):
        xl2, y2 = lax.rem(xl + lax.rem(j, 2), 2), lax.rem(y + j // 2, 4)
        return ((xl2 * 4 + y2) * 2 + core, mp), y2 * 2 + xl2

    def plane_peer(j):
        return plane_dev(lax.rem(x + lax.rem(j, 4), 4), lax.rem(y + j // 4, 4))

    def copy(src, dst, phase, device, recv=None):
        return pltpu.make_async_remote_copy(
            src_ref=src, dst_ref=dst, send_sem=ssem.at[phase],
            recv_sem=rsem.at[phase] if recv is None else recv, device_id=device, device_id_type=MESH,
        )

    def got(ref, phase):
        copy(ref, ref, phase, partner).wait_recv()

    def sent(ref, phase):
        copy(ref, ref, phase, partner).wait_send()

    barrier = pltpu.get_barrier_semaphore()

    def greet(j, _):
        pl.semaphore_signal(barrier, inc=1, device_id=mp_peer(j), device_id_type=MESH)
        pl.semaphore_signal(barrier, inc=1, device_id=plane_peer(j), device_id_type=MESH)
        return 0

    lax.fori_loop(1, 16, greet, 0)
    pl.semaphore_signal(barrier, inc=1, device_id=partner, device_id_type=MESH)

    own_slot = y * 4 + x
    own_text = rows_at(own_slot * OWN, OWN, OWN)
    wide = t_ref[...].astype(F32)
    txt[own_text, :D] = (wide / row_norm(wide)).astype(BF16)
    eye = lax.broadcasted_iota(jnp.int32, (OWN, OWN), 0) == lax.broadcasted_iota(jnp.int32, (OWN, OWN), 1)
    tb_col = jnp.sum(jnp.where(eye, tb_ref[...].astype(F32), 0.0), axis=1, keepdims=True)
    lane = lax.broadcasted_iota(jnp.int32, (OWN, ext), 1)
    level = jnp.where(lane < 24, lax.rem(lane, 8), -1).astype(F32)
    txt[own_text, D:] = jnp.where(level == tb_col, 1.0, 0.0).astype(BF16)

    pos = pos_ref[...]
    pos_hi = pos // 64
    line = lax.broadcasted_iota(jnp.int32, (8, ROWS), 0)
    table_rows = jnp.where(
        line == 0, pos_hi, jnp.where(line == 1, pos - pos_hi * 64, jnp.where(line == 2, ib_ref[...], 0))
    ).astype(F32).astype(BF16)
    took = lax.broadcasted_iota(jnp.int32, (ROWS, 256), 0)
    into = lax.broadcasted_iota(jnp.int32, (ROWS, 256), 1)
    pick = jnp.where(took == (into // 32) * 64 + xh * 32 + lax.rem(into, 32), 1.0, 0.0).astype(BF16)
    meta[core] = dot(table_rows, pick)

    pl.semaphore_wait(barrier, 31)

    def send_text(j, _):
        copy(txt.at[own_text], txt.at[own_text], TEXT, plane_peer(j)).start()
        return 0

    lax.fori_loop(1, 16, send_text, 0)
    copy(meta.at[core], meta.at[core], META, partner).start()

    def forward(t, _):
        b = lax.rem(mp // 4 + 1 + t, 4)
        rows = rows_at(b * 128, 128, 128)
        pre = dot(x_ref[rows, :], wi_ref[...])
        hp[rows, :] = pre
        a = gelu_tanh(pre).astype(BF16)
        act[rows, :] = a
        rs1s[rows, :] = dot(a, wo_ref[...]).astype(BF16)

        def send(i, _):
            k = b * 4 + i
            j = lax.rem(k - mp + 16, 16)

            @pl.when(j != 0)
            def _():
                copy(
                    rs1s.at[rows_at(k * OWN, OWN, OWN)], rs1r.at[rows_at((j - 1) * OWN, OWN, OWN)], RS1, (dp, k)
                ).start()

            return 0

        lax.fori_loop(0, 4, send, 0)
        return 0

    lax.fori_loop(0, 4, forward, 0)
    own_rows = rows_at(mp * OWN, OWN, OWN)
    features = x_ref[own_rows, :].astype(F32) + dot(act[own_rows, :], wo_ref[...])
    got(rs1r, RS1)

    def add_rs1(j, total):
        return total + rs1r[rows_at(j * OWN, OWN, OWN), :].astype(F32)

    features = lax.fori_loop(0, 15, add_rs1, features)
    norm = row_norm(features)
    unit = features / norm

    own_img = rows_at((core * 8 + z) * OWN, OWN, OWN)
    img[own_img, :] = unit.astype(BF16)

    def send_img(j, _):
        copy(img.at[own_img], img.at[own_img], AG1Z, z_peer(j), zsem.at[j - 1]).start()
        return 0

    lax.fori_loop(1, 8, send_img, 0)
    copy(img.at[own_img], img.at[own_img], AG1C, partner).start()

    got(meta.at[1 - core], META)

    def table_of(half):
        m = meta[half]
        bucket = m[2:3, :]
        w = jnp.zeros((8, 256), F32)
        for k in range(8):
            w = w + jnp.where(bucket == float(k), tab_ref[:, k : k + 1], 0.0)
        hi = w.astype(BF16).astype(F32)
        mid = (w - hi).astype(BF16).astype(F32)
        low = w - hi - mid
        return jnp.concatenate([hi, mid, low, jnp.zeros((ext - 24, 256), F32)], axis=0).astype(BF16)

    hot[0] = table_of(core)
    hot[1] = table_of(1 - core)
    match = [m[0:1, :] * 64.0 + m[1:2, :] for m in (meta[core], meta[1 - core])]
    got(txt.at[pl.ds(0, 15 * OWN)], TEXT)

    def forward_img(j, _):
        slot = rows_at((core * 8 + lax.rem(z - j + 8, 8)) * OWN, OWN, OWN)
        copy(img.at[slot], img.at[slot], AG1Z, partner, zsem.at[j - 1]).wait_recv()
        copy(img.at[slot], img.at[slot], AG1C, partner).start()
        return 0

    lax.fori_loop(1, 8, forward_img, 0)

    loss_acc[...] = jnp.zeros_like(loss_acc)

    def pairs(half):
        images = rows_at((core if half == 0 else 1 - core) * 256, 256, 256)

        def step(b, _):
            rows = rows_at(b * 128, 128, 128)
            logits = logit_scale * dot_nt(txt[rows, :D], img[images, :]) + logit_bias
            weight = dot(txt[rows, D:], hot[half])
            slot = b * 128 + lax.broadcasted_iota(jnp.int32, (128, 256), 0)
            p = slot // OWN
            px, py = lax.rem(p, 4), p // 4
            index = (((lax.rem(px, 2) * 4 + py) * 2 + core) * 16 + z * 2 + px // 2) * OWN + lax.rem(slot, OWN)
            hit = index.astype(F32) == match[half]
            against = jnp.where(hit, -logits, logits)
            grown = jnp.exp(against)
            loss_acc[...] += weight * jnp.log(1.0 + grown)
            slope = logit_scale * weight * (grown / (1.0 + grown))
            coef[half, rows, :] = jnp.where(hit, -slope, slope).astype(BF16)
            return 0

        lax.fori_loop(0, 4, step, 0)

    pairs(0)
    got(img.at[pl.ds(0, 8 * OWN)], AG1C)
    pairs(1)

    for b in range(2):
        rows = pl.ds(b * 128, 128)
        c_send[rows, :] = dot_tn(coef[1, :, b * 128 : b * 128 + 128], txt[:, :D]).astype(BF16)
        copy(c_send.at[rows], c_recv.at[rows], RS2C, partner).start()
    for b in range(2):
        rows = pl.ds(b * 128, 128)
        ig[rows, :] = dot_tn(coef[0, :, b * 128 : b * 128 + 128], txt[:, :D])
    got(c_recv, RS2C)

    def send_rs2(j, _):
        rows = rows_at(lax.rem(z + j, 8) * OWN, OWN, OWN)
        rs2s[rows, :] = (ig[rows, :] + c_recv[rows, :].astype(F32)).astype(BF16)
        copy(rs2s.at[rows], rs2r.at[rows_at((j - 1) * OWN, OWN, OWN)], RS2Z, z_peer(j)).start()
        return 0

    lax.fori_loop(1, 8, send_rs2, 0)

    own_half, other_half = rows_at(core * 256, 256, 256), rows_at((1 - core) * 256, 256, 256)

    def text_grad(t, _):
        b = lax.rem(y + 1 + t, 4)
        rows = rows_at(b * 128, 128, 128)
        tgs[rows, :] = (dot(coef[0, rows, :], img[own_half, :]) + dot(coef[1, rows, :], img[other_half, :])).astype(BF16)

        def send(i, _):
            j = lax.rem(b - y + 4, 4) * 4 + lax.rem(i - x + 4, 4)

            @pl.when(j != 0)
            def _():
                copy(
                    tgs.at[rows_at((b * 4 + i) * OWN, OWN, OWN)], tgr.at[rows_at((j - 1) * OWN, OWN, OWN)], TG,
                    plane_dev(i, b),
                ).start()

            return 0

        lax.fori_loop(0, 4, send, 0)
        return 0

    lax.fori_loop(0, 4, text_grad, 0)
    l_tile[...] = jnp.zeros((8, 128), F32) + jnp.sum(loss_acc[...])

    def send_loss(j, _):
        copy(l_tile, l1r.at[rows_at((j - 1) * 8, 8, 8)], LOSS1, plane_peer(j)).start()
        return 0

    lax.fori_loop(1, 16, send_loss, 0)
    grad_text = dot(coef[0, own_text, :], img[own_half, :]) + dot(coef[1, own_text, :], img[other_half, :])

    own_z = rows_at(z * OWN, OWN, OWN)
    own_grad = ig[own_z, :] + c_recv[own_z, :].astype(F32)
    got(rs2r, RS2Z)

    def add_rs2(j, total):
        return total + rs2r[rows_at(j * OWN, OWN, OWN), :].astype(F32)

    own_grad = lax.fori_loop(0, 7, add_rs2, own_grad)
    projected = jnp.sum(unit * own_grad, axis=-1, keepdims=True)
    grad_features = (own_grad - unit * projected) / norm
    gfall[own_rows, :] = grad_features.astype(BF16)

    def send_gf(j, _):
        copy(gfall.at[own_rows], gfall.at[own_rows], AG2, mp_peer(j)).start()
        return 0

    lax.fori_loop(1, 16, send_gf, 0)

    got(l1r, LOSS1)
    loss = l_tile[...]
    for j in range(15):
        loss = loss + l1r[j * 8 : j * 8 + 8, :]
    lc_tile[...] = loss
    copy(lc_tile, lcr, LOSSC, partner).start()
    got(tgr, TG)

    def add_tg(j, total):
        return total + tgr[rows_at(j * OWN, OWN, OWN), :].astype(F32)

    gt_ref[...] = lax.fori_loop(0, 15, add_tg, grad_text)
    got(lcr, LOSSC)
    lz_tile[...] = loss + lcr[...]

    def send_loss_z(j, _):
        copy(lz_tile, lzr.at[rows_at((j - 1) * 8, 8, 8)], LOSSZ, z_peer(j)).start()
        return 0

    lax.fori_loop(1, 8, send_loss_z, 0)
    got(gfall.at[pl.ds(0, 15 * OWN)], AG2)

    def backward(t, _):
        b = lax.rem(mp // 4 + 1 + t, 4)
        rows = rows_at(b * 128, 128, 128)
        g = (dot_nt(gfall[rows, :], wo_ref[...]) * gelu_slope(hp[rows, :])).astype(BF16)
        gh[rows, :] = g
        rs3s[rows, :] = dot_nt(g, wi_ref[...]).astype(BF16)

        def send(i, _):
            k = b * 4 + i
            j = lax.rem(k - mp + 16, 16)

            @pl.when(j != 0)
            def _():
                copy(
                    rs3s.at[rows_at(k * OWN, OWN, OWN)], rs3r.at[rows_at((j - 1) * OWN, OWN, OWN)], RS3, (dp, k)
                ).start()

            return 0

        lax.fori_loop(0, 4, send, 0)
        return 0

    lax.fori_loop(0, 4, backward, 0)

    other_cols, own_cols = rows_at((1 - core) * 128, 128, 128), rows_at(core * 128, 128, 128)

    def w_in_half(cols, out, kind):
        def step(b, _):
            part = rows_at(b * 128, 128, 128)
            out[part, :] = dot_tn(x_ref[:, part], gh[:, cols]).astype(kind)
            return 0

        lax.fori_loop(0, 9, step, 0)

    arc_so[...] = dot_tn(act[:, other_cols], gfall[...]).astype(BF16)
    copy(arc_so, arc_ro, ARC_O, partner).start()
    w_in_half(other_cols, arc_si, BF16)
    copy(arc_si, arc_ri, ARC_I, partner).start()
    awo[...] = dot_tn(act[:, own_cols], gfall[...])
    w_in_half(own_cols, awi, F32)
    got(arc_ro, ARC_O)
    awo[...] += arc_ro[...].astype(F32)
    ars_so[...] = awo[...].astype(BF16)
    got(arc_ri, ARC_I)
    awi[...] += arc_ri[...].astype(F32)
    ars_si[...] = awi[...].astype(BF16)

    def send_ars(j, _):
        device, q = ar_peer(j)
        copy(ars_si.at[rows_at(q * 144, 144, 144)], ars_ri.at[rows_at((j - 1) * 144, 144, 144)], ARS_I, device).start()
        copy(ars_so.at[rows_at(q * 16, 16, 16)], ars_ro.at[rows_at((j - 1) * 16, 16, 16)], ARS_O, device).start()
        return 0

    lax.fori_loop(1, 8, send_ars, 0)
    q = y * 2 + xl
    own_in, own_out = rows_at(q * 144, 144, 144), rows_at(q * 16, 16, 16)
    total_in, total_out = awi[own_in, :], awo[own_out, :]
    got(ars_ri, ARS_I)
    for j in range(7):
        total_in = total_in + ars_ri[j * 144 : j * 144 + 144, :].astype(F32)
    got(ars_ro, ARS_O)
    for j in range(7):
        total_out = total_out + ars_ro[j * 16 : j * 16 + 16, :].astype(F32)
    fwi[core, own_in, :] = total_in.astype(BF16)
    fwo[core, own_out, :] = total_out.astype(BF16)

    def send_aag(j, _):
        device, _ = ar_peer(j)
        copy(fwi.at[core, own_in], fwi.at[core, own_in], AAG_I, device).start()
        copy(fwo.at[core, own_out], fwo.at[core, own_out], AAG_O, device).start()
        return 0

    lax.fori_loop(1, 8, send_aag, 0)

    got(lzr, LOSSZ)
    loss = lz_tile[...]
    for j in range(7):
        loss = loss + lzr[j * 8 : j * 8 + 8, :]
    loss_ref[...] = loss * (1.0 / PAIRS)
    grad_image = grad_features + dot_nt(gh[own_rows, :], wi_ref[...])

    got(fwi.at[core, pl.ds(0, 7 * 144)], AAG_I)
    copy(fwi.at[core], fwi.at[core], AFC_I, partner).start()
    got(fwo.at[core, pl.ds(0, 7 * 16)], AAG_O)
    copy(fwo.at[core], fwo.at[core], AFC_O, partner).start()
    got(rs3r, RS3)

    def add_rs3(j, total):
        return total + rs3r[rows_at(j * OWN, OWN, OWN), :].astype(F32)

    gi_ref[...] = lax.fori_loop(0, 15, add_rs3, grad_image)
    got(fwi.at[1 - core], AFC_I)
    for half in range(2):
        gwi_ref[:, half * 128 : half * 128 + 128] = fwi[half]
    got(fwo.at[1 - core], AFC_O)
    for half in range(2):
        gwo_ref[half * 128 : half * 128 + 128, :] = fwo[half]

    sent(txt.at[pl.ds(0, 15 * OWN)], TEXT)
    sent(meta.at[0], META)
    sent(rs1r, RS1)
    sent(img.at[pl.ds(0, 7 * OWN)], AG1Z)
    sent(img.at[pl.ds(0, 8 * OWN)], AG1C)
    sent(c_send, RS2C)
    sent(rs2r, RS2Z)
    sent(tgr, TG)
    sent(l1r, LOSS1)
    sent(lc_tile, LOSSC)
    sent(lzr, LOSSZ)
    sent(gfall.at[pl.ds(0, 15 * OWN)], AG2)
    sent(rs3r, RS3)
    sent(arc_si, ARC_I)
    sent(arc_so, ARC_O)
    sent(ars_ri, ARS_I)
    sent(ars_ro, ARS_O)
    sent(fwi.at[0, pl.ds(0, 7 * 144)], AAG_I)
    sent(fwo.at[0, pl.ds(0, 7 * 16)], AAG_O)
    sent(fwi.at[0], AFC_I)
    sent(fwo.at[0], AFC_O)


def per_device(
    image_feats, text_feats, w_in, w_out, image_bucket, text_bucket, positive, reward_table
):
    vmem = pl.BlockSpec(memory_space=pltpu.VMEM)

    def buf(shape, kind=BF16):
        return pltpu.VMEM(shape, kind)

    scratch = [
        buf((ROWS, HID), F32),
        buf((ROWS, HID)),
        buf((ROWS, D)),
        buf((15 * OWN, D)),
        buf((ROWS, D + ext)),
        buf((2, 8, 256), F32),
        buf((2, ext, 256)),
        buf((ROWS, D)),
        buf((2, ROWS, 256)),
        buf((128, 256), F32),
        buf((256, D)),
        buf((256, D)),
        buf((256, D), F32),
        buf((256, D)),
        buf((7 * OWN, D)),
        buf((ROWS, D)),
        buf((15 * OWN, D)),
        buf((8, 128), F32),
        buf((15 * 8, 128), F32),
        buf((8, 128), F32),
        buf((8, 128), F32),
        buf((8, 128), F32),
        buf((7 * 8, 128), F32),
        buf((ROWS, D)),
        buf((ROWS, HID)),
        buf((ROWS, D)),
        buf((15 * OWN, D)),
        buf((D, 128)),
        buf((128, D)),
        buf((D, 128)),
        buf((128, D)),
        buf((D, 128), F32),
        buf((128, D), F32),
        buf((D, 128)),
        buf((128, D)),
        buf((7 * 144, 128)),
        buf((7 * 16, D)),
        buf((2, D, 128)),
        buf((2, 128, D)),
        pltpu.SemaphoreType.DMA((21,)),
        pltpu.SemaphoreType.DMA((21,)),
        pltpu.SemaphoreType.DMA((7,)),
    ]
    loss, grad_text, grad_image, grad_w_in, grad_w_out = pl.pallas_call(
        kernel,
        out_shape=(
            jax.ShapeDtypeStruct((8, 128), F32),
            jax.ShapeDtypeStruct((OWN, D), F32),
            jax.ShapeDtypeStruct((OWN, D), F32),
            jax.ShapeDtypeStruct((D, HID), BF16),
            jax.ShapeDtypeStruct((HID, D), BF16),
        ),
        in_specs=[vmem] * 8,
        out_specs=(vmem,) * 5,
        scratch_shapes=scratch,
        compiler_params=pltpu.CompilerParams(
            collective_id=0, has_side_effects=True, vmem_limit_bytes=VMEM_LIMIT
        ),
        name="pairs_and_block",
    )(
        image_feats, text_feats, w_in, w_out, image_bucket[None, :], text_bucket[None, :], positive[None, :],
        reward_table.T,
    )
    return (loss[0, 0], grad_text, grad_image, grad_w_in.astype(F32), grad_w_out.astype(F32))


def solution(mesh):
    return jax.shard_map(
        per_device,
        mesh=mesh,
        in_specs=(
            P("dp", None),
            P(("dp", "mp"), None),
            P(None, "mp"),
            P("mp", None),
            P("dp"),
            P(("dp", "mp")),
            P("dp"),
            P(),
        ),
        out_specs=(P(), P(("dp", "mp"), None), P(("dp", "mp"), None), P(None, "mp"), P("mp", None)),
        check_vma=False,
    )
```

time: 1120 us -> 154 us (0.14)
  waiting for transfers between devices: 830 us -> 0 us
  Pallas kernels: 0 us -> 142 us
  matrix products: 113 us -> 0 us
  blocking collectives: 79.3 us -> 0 us
  starting transfers between devices: 49.6 us -> 0 us
  between operations: 16.1 us -> 0.65 us
  loops' own time: 11.5 us -> 0 us
    reduce_scatter x3 -> x0, waiting for transfers between devices: 627 us -> none  [the longest x1 211 us: per_device(): lax.psum_scatter(jnp.dot(activation, w_out, preferred_element_type=jnp.fl...]
    all_gather x2 -> x0, waiting for transfers between devices: 156 us -> none  [the longest x1 78.1 us: per_device(): lax.all_gather(unit_own.astype(jnp.bfloat16), 'mp', axis=0, tiled=True)]
    pallas_call x0 -> x1, Pallas kernels: none -> 142 us  [per_device(): pl.pallas_call(kernel, out_shape=(jax.ShapeDtypeStruct((8, 128), F32), ja...]
    dot_general x71 -> x0, matrix products: 113 us -> none  [the longest x16 55.5 us: turn(): lax.dot_general(coefficient, text_block, (((0,), (0,)), ((), ())), prefer...]
    psum x1 -> x0, blocking collectives: 79.3 us -> none  [per_device(): pair_loss = lax.psum(loss_sum, ('dp', 'mp')) / (pair_count * pair_count)]
    ppermute x48 -> x0, starting transfers between devices: 49.3 us -> none  [from_behind(): return lax.ppermute(value, axis, pairs)]
    psum x1 -> x0, waiting for transfers between devices: 46.6 us -> none  [per_device(): grad_w_in, grad_w_out = lax.psum((local_w_in, local_w_out), 'dp')]
    another operation x1 -> x0, loops' own time: 11.5 us -> none  [per_device(): final_state = lax.fori_loop(0, loop_size, turn, start_state)]
  transfers between devices with their start and end apart: 54 -> 0, of which waited for: 6 -> 0; matrix products, arithmetic and copies ran while one was open for 10% -> 0% of each run, Pallas kernels for 0% -> 0%
where the time goes in v1:
time: 154 us; the launch traced here: 153 us
  Pallas kernels  142 us (92%)
  local copies, waits for them, and re-layouts  8.89 us (6%)
  other arithmetic  2.19 us (1%)
    pallas_call x1, Pallas kernels, per_device(): pl.pallas_call(kernel, out_shape=(jax.ShapeDtypeStruct((8, 128), F32), ja...  142 us
    unnamed x17, local copies, waits for them, and re-layouts  8.38 us

profile of v1, /device:TPU:1, one launch (start us, length us, event | category | flops | bytes accessed | tf_op | source)
XLA Modules:
  0.0 153.4 jit_solution(15663946179014041247)
XLA Ops:
  0.6 0.8 copy.13
  1.4 0.0 copy-start
  1.4 1.3 copy-done
  2.7 0.0 copy-start.1
  2.7 1.1 copy-done.1
  3.7 0.0 copy-start.2
  3.7 1.1 copy-done.2
  4.8 0.0 copy-start.3
  4.8 0.9 copy-done.3
  5.7 0.0 copy-start.4
  5.7 0.7 copy-done.4
  6.4 0.0 copy-start.5
  6.4 0.7 copy-done.5
  7.0 0.0 copy-start.6
  7.0 0.7 copy-done.6
  7.7 141.6 %pairs_and_block.1 = (f32[8,128]{1,0:T(8,128)S(1)}, f32[32,1152]{1,0:T(8,128)S(1)}, f32[32,1152]{1,0:T(8,128)S(1)}, bf16[1152,256]{1,0:T(8,128)(2,1)S(1)}, bf16[256,1152]{1,0:T(8,128)(2,1)S(1)}) custom-call(bf16[512,1152]{1,0:T(8,128)(2,1)S(1)} %copy-done, bf16[32,1152]{1,0:T(8,128)(2,1)S(1)} %copy-done.3, bf16[1152,256]{1,0:T(8,128)(2,1)S(1)} %copy-done.1, ...), custom_call_target="tpu_custom_call" | custom-call | tf_op jit(solution)/shard_map/pairs_and_block/pallas_call | solution.py:506
  149.3 0.5 slice.3
  149.8 1.1 convert_element_type.6
  150.9 1.1 convert_element_type.7
  152.0 0.7 copy.16
  152.7 0.7 copy.17
Async XLA Ops:
  1.4 1.3 copy-start
  2.7 1.1 copy-start.1
  3.7 1.1 copy-start.2
  4.8 0.9 copy-start.3
  5.7 0.7 copy-start.4
  6.4 0.7 copy-start.5
  7.0 0.7 copy-start.6

commit v2 on v1

--- a/solution.py
+++ b/solution.py
@@ -52,8 +52,10 @@
     return jnp.sqrt(jnp.sum(v * v, axis=-1, keepdims=True) + norm_eps)
 
 
-(TEXT, META, RS1, AG1C, RS2C, RS2Z, TG, LOSS1, LOSSC, LOSSZ, AG2, RS3, ARC_I, ARC_O, ARS_I, ARS_O, AAG_I, AAG_O,
- AFC_I, AFC_O, AG1Z) = range(21)
+(TEXT, META, RS1, RS1X, AG1C, RS2C, RS2Z, TG, LOSS1, LOSSC, LOSSZ, AG2, AG2X, RS3, RS3X, ARC_I, ARC_O, ARS_I, ARS_O,
+ AAG_I, AAG_O, AFC_I, AFC_O, AG1Z) = range(24)
+FLOW = 16
+UP, DOWN = 0, 1
 
 
 def rows_at(start, count, step):
@@ -61,12 +63,13 @@
 
 
 def kernel(
+    x_hbm, t_hbm, wi_hbm, wo_hbm, ib_hbm, tb_hbm, pos_hbm, tab_hbm,
+    loss_ref, gt_ref, gi_ref, gwi_ref, gwo_ref,
     x_ref, t_ref, wi_ref, wo_ref, ib_ref, tb_ref, pos_ref, tab_ref,
-    loss_ref, gt_ref, gi_ref, gwi_ref, gwo_ref,
-    hp, act, rs1s, rs1r, txt, meta, hot, img, coef, loss_acc, c_send, c_recv, ig, rs2s, rs2r, tgs, tgr,
-    l_tile, l1r, lc_tile, lcr, lz_tile, lzr, gfall, gh, rs3s, rs3r,
+    hp, act, part, rs1s, rs1r, rs1xs, rs1xr, txt, meta, hot, img, coef, loss_acc, c_send, c_recv, ig, rs2s, rs2r, tgs, tgr,
+    l_tile, l1r, lc_tile, lcr, lz_tile, lzr, gfall, gh, rs3s, rs3r, rs3xs, rs3xr,
     arc_si, arc_so, arc_ri, arc_ro, awi, awo, ars_si, ars_so, ars_ri, ars_ro, fwi, fwo,
-    ssem, rsem, zsem,
+    lsem, ssem, rsem, zsem, rs1sem, ag2sem, rs3sem,
 ):
     dp, mp = lax.axis_index("dp"), lax.axis_index("mp")
     core, y, xl = lax.rem(dp, 2), lax.rem(dp // 2, 4), dp // 8
@@ -74,8 +77,7 @@
     x = xh * 2 + xl
     partner = (dp + 1 - 2 * core, mp)
 
-    def mp_peer(j):
-        return (dp, lax.rem(mp + j, 16))
+    across = (dp, mp + 1 - 2 * xh)
 
     def z_peer(j):
         return (dp, lax.rem(z + j, 8) * 2 + xh)
@@ -105,12 +107,31 @@
     barrier = pltpu.get_barrier_semaphore()
 
     def greet(j, _):
-        pl.semaphore_signal(barrier, inc=1, device_id=mp_peer(j), device_id_type=MESH)
         pl.semaphore_signal(barrier, inc=1, device_id=plane_peer(j), device_id_type=MESH)
         return 0
 
     lax.fori_loop(1, 16, greet, 0)
+
+    def greet_z(j, _):
+        pl.semaphore_signal(barrier, inc=1, device_id=z_peer(j), device_id_type=MESH)
+        return 0
+
+    lax.fori_loop(1, 8, greet_z, 0)
     pl.semaphore_signal(barrier, inc=1, device_id=partner, device_id_type=MESH)
+
+    loads = [
+        pltpu.make_async_copy(src, dst, lsem.at[i])
+        for i, (src, dst) in enumerate(
+            (
+                (t_hbm, t_ref), (tb_hbm, tb_ref), (pos_hbm, pos_ref), (ib_hbm, ib_ref), (tab_hbm, tab_ref),
+                (x_hbm, x_ref), (wi_hbm, wi_ref), (wo_hbm, wo_ref),
+            )
+        )
+    ]
+    for load in loads:
+        load.start()
+    for load in loads[:5]:
+        load.wait()
 
     own_slot = y * 4 + x
     own_text = rows_at(own_slot * OWN, OWN, OWN)
@@ -133,7 +154,7 @@
     pick = jnp.where(took == (into // 32) * 64 + xh * 32 + lax.rem(into, 32), 1.0, 0.0).astype(BF16)
     meta[core] = dot(table_rows, pick)
 
-    pl.semaphore_wait(barrier, 31)
+    pl.semaphore_wait(barrier, 23)
 
     def send_text(j, _):
         copy(txt.at[own_text], txt.at[own_text], TEXT, plane_peer(j)).start()
@@ -142,39 +163,89 @@
     lax.fori_loop(1, 16, send_text, 0)
     copy(meta.at[core], meta.at[core], META, partner).start()
 
-    def forward(t, _):
-        b = lax.rem(mp // 4 + 1 + t, 4)
-        rows = rows_at(b * 128, 128, 128)
+    def hops(f, way):
+        return 4 if f % 2 == way else 3
+
+    def slot_of(f, way, far, flows):
+        return pl.ds(((way * flows + f) * 4 + far - 1) * FLOW, FLOW)
+
+    def neighbour(way):
+        return z_peer(1 if way == UP else 7)
+
+    def toward(way, far):
+        return lax.rem(z + (far if way == UP else 8 - far), 8)
+
+    def reduce_step(far, flows, row_of, held, sbuf, rbuf, phase, sems):
+        for f in range(flows):
+            for way in (UP, DOWN):
+                if far > hops(f, way):
+                    continue
+                value = held[rows_at(row_of(f, toward(way, far)), FLOW, FLOW), :]
+                if far < hops(f, way):
+                    before = slot_of(f, way, far + 1, flows)
+                    sem = sems.at[(way * flows + f) * 4 + far]
+                    copy(rbuf.at[before], rbuf.at[before], phase, partner, sem).wait_recv()
+                    value = value + rbuf[before, :].astype(F32)
+                slot = slot_of(f, way, far, flows)
+                sbuf[slot, :] = value.astype(BF16)
+                sem = sems.at[(way * flows + f) * 4 + far - 1]
+                copy(sbuf.at[slot], rbuf.at[slot], phase, neighbour(way), sem).start()
+
+    def reduce_end(f, flows, row_of, held, rbuf, phase, sems):
+        value = held[rows_at(row_of(f, z), FLOW, FLOW), :]
+        for way in (UP, DOWN):
+            slot = slot_of(f, way, 1, flows)
+            copy(rbuf.at[slot], rbuf.at[slot], phase, partner, sems.at[(way * flows + f) * 4]).wait_recv()
+            value = value + rbuf[slot, :].astype(F32)
+        return value
+
+    def gather_step(far, flows, row_of, buf, phase, sems):
+        for f in flows:
+            for way in (UP, DOWN):
+                if far > hops(f, way):
+                    continue
+                rows = rows_at(row_of(f, toward(1 - way, far - 1)), FLOW, FLOW)
+                if far > 1:
+                    sem = sems.at[(way * 4 + f) * 4 + far - 2]
+                    copy(buf.at[rows], buf.at[rows], phase, partner, sem).wait_recv()
+                sem = sems.at[(way * 4 + f) * 4 + far - 1]
+                copy(buf.at[rows], buf.at[rows], phase, neighbour(way), sem).start()
+
+    def gather_end(flows, row_of, buf, phase, sems):
+        for f in flows:
+            for way in (UP, DOWN):
+                rows = rows_at(row_of(f, toward(1 - way, hops(f, way))), FLOW, FLOW)
+                sem = sems.at[(way * 4 + f) * 4 + hops(f, way) - 1]
+                copy(buf.at[rows], buf.at[rows], phase, partner, sem).wait_recv()
+
+    def mp_row(f, z2):
+        return (z2 * 2 + (1 - xh if f < 2 else xh)) * OWN + (f % 2) * FLOW
+
+    for load in loads[5:]:
+        load.wait()
+
+    def forward(z2):
+        rows = rows_at(z2 * 64, 64, 64)
         pre = dot(x_ref[rows, :], wi_ref[...])
         hp[rows, :] = pre
         a = gelu_tanh(pre).astype(BF16)
         act[rows, :] = a
-        rs1s[rows, :] = dot(a, wo_ref[...]).astype(BF16)
-
-        def send(i, _):
-            k = b * 4 + i
-            j = lax.rem(k - mp + 16, 16)
-
-            @pl.when(j != 0)
-            def _():
-                copy(
-                    rs1s.at[rows_at(k * OWN, OWN, OWN)], rs1r.at[rows_at((j - 1) * OWN, OWN, OWN)], RS1, (dp, k)
-                ).start()
-
-            return 0
-
-        lax.fori_loop(0, 4, send, 0)
-        return 0
-
-    lax.fori_loop(0, 4, forward, 0)
+        part[rows, :] = dot(a, wo_ref[...])
+
+    forward(toward(UP, 4))
+    for far in (4, 3, 2, 1):
+        reduce_step(far, 4, mp_row, part, rs1s, rs1r, RS1, rs1sem)
+        forward(toward(UP, far - 1))
+        if far > 1:
+            forward(toward(DOWN, far - 1))
     own_rows = rows_at(mp * OWN, OWN, OWN)
-    features = x_ref[own_rows, :].astype(F32) + dot(act[own_rows, :], wo_ref[...])
-    got(rs1r, RS1)
-
-    def add_rs1(j, total):
-        return total + rs1r[rows_at(j * OWN, OWN, OWN), :].astype(F32)
-
-    features = lax.fori_loop(0, 15, add_rs1, features)
+    for f in (0, 1):
+        rs1xs[f * FLOW : f * FLOW + FLOW, :] = reduce_end(f, 4, mp_row, part, rs1r, RS1, rs1sem).astype(BF16)
+    copy(rs1xs, rs1xr, RS1X, across).start()
+    features = jnp.concatenate([reduce_end(f, 4, mp_row, part, rs1r, RS1, rs1sem) for f in (2, 3)], axis=0)
+    features = features + x_ref[own_rows, :].astype(F32)
+    got(rs1xr, RS1X)
+    features = features + rs1xr[...].astype(F32)
     norm = row_norm(features)
     unit = features / norm
 
@@ -189,13 +260,16 @@
     copy(img.at[own_img], img.at[own_img], AG1C, partner).start()
 
     got(meta.at[1 - core], META)
+
+    eye8 = lax.broadcasted_iota(jnp.int32, (8, 8), 0) == lax.broadcasted_iota(jnp.int32, (8, 8), 1)
 
     def table_of(half):
         m = meta[half]
         bucket = m[2:3, :]
         w = jnp.zeros((8, 256), F32)
         for k in range(8):
-            w = w + jnp.where(bucket == float(k), tab_ref[:, k : k + 1], 0.0)
+            column = jnp.sum(jnp.where(eye8, tab_ref[k : k + 1, :], 0.0), axis=1, keepdims=True)
+            w = w + jnp.where(bucket == float(k), column, 0.0)
         hi = w.astype(BF16).astype(F32)
         mid = (w - hi).astype(BF16).astype(F32)
         low = w - hi - mid
@@ -302,11 +376,14 @@
     grad_features = (own_grad - unit * projected) / norm
     gfall[own_rows, :] = grad_features.astype(BF16)
 
-    def send_gf(j, _):
-        copy(gfall.at[own_rows], gfall.at[own_rows], AG2, mp_peer(j)).start()
-        return 0
-
-    lax.fori_loop(1, 16, send_gf, 0)
+    across_rows = rows_at((mp + 1 - 2 * xh) * OWN, OWN, OWN)
+    copy(gfall.at[own_rows], gfall.at[own_rows], AG2X, across).start()
+    gather_step(1, (2, 3), mp_row, gfall, AG2, ag2sem)
+
+    got(gfall.at[across_rows], AG2X)
+    gather_step(1, (0, 1), mp_row, gfall, AG2, ag2sem)
+    gather_step(2, (2, 3, 0, 1), mp_row, gfall, AG2, ag2sem)
+    gather_step(3, (2, 3, 0, 1), mp_row, gfall, AG2, ag2sem)
 
     got(l1r, LOSS1)
     loss = l_tile[...]
@@ -328,31 +405,25 @@
         return 0
 
     lax.fori_loop(1, 8, send_loss_z, 0)
-    got(gfall.at[pl.ds(0, 15 * OWN)], AG2)
-
-    def backward(t, _):
-        b = lax.rem(mp // 4 + 1 + t, 4)
+    gather_step(4, (2, 3, 0, 1), mp_row, gfall, AG2, ag2sem)
+    gather_end((2, 3, 0, 1), mp_row, gfall, AG2, ag2sem)
+
+    def backward(b, _):
         rows = rows_at(b * 128, 128, 128)
-        g = (dot_nt(gfall[rows, :], wo_ref[...]) * gelu_slope(hp[rows, :])).astype(BF16)
-        gh[rows, :] = g
-        rs3s[rows, :] = dot_nt(g, wi_ref[...]).astype(BF16)
-
-        def send(i, _):
-            k = b * 4 + i
-            j = lax.rem(k - mp + 16, 16)
-
-            @pl.when(j != 0)
-            def _():
-                copy(
-                    rs3s.at[rows_at(k * OWN, OWN, OWN)], rs3r.at[rows_at((j - 1) * OWN, OWN, OWN)], RS3, (dp, k)
-                ).start()
-
-            return 0
-
-        lax.fori_loop(0, 4, send, 0)
+        gh[rows, :] = (dot_nt(gfall[rows, :], wo_ref[...]) * gelu_slope(hp[rows, :])).astype(BF16)
         return 0
 
     lax.fori_loop(0, 4, backward, 0)
+
+    def to_input(z2):
+        rows = rows_at(z2 * 64, 64, 64)
+        part[rows, :] = dot_nt(gh[rows, :], wi_ref[...])
+
+    def rs3_step(far):
+        reduce_step(far, 4, mp_row, part, rs3s, rs3r, RS3, rs3sem)
+        to_input(toward(UP, far - 1))
+        if far > 1:
+            to_input(toward(DOWN, far - 1))
 
     other_cols, own_cols = rows_at((1 - core) * 128, 128, 128), rows_at(core * 128, 128, 128)
 
@@ -369,68 +440,88 @@
     w_in_half(other_cols, arc_si, BF16)
     copy(arc_si, arc_ri, ARC_I, partner).start()
     awo[...] = dot_tn(act[:, own_cols], gfall[...])
-    w_in_half(own_cols, awi, F32)
     got(arc_ro, ARC_O)
     awo[...] += arc_ro[...].astype(F32)
     ars_so[...] = awo[...].astype(BF16)
+
+    def send_ars_out(j, _):
+        device, q = ar_peer(j)
+        copy(ars_so.at[rows_at(q * 16, 16, 16)], ars_ro.at[rows_at((j - 1) * 16, 16, 16)], ARS_O, device).start()
+        return 0
+
+    lax.fori_loop(1, 8, send_ars_out, 0)
+    w_in_half(own_cols, awi, F32)
     got(arc_ri, ARC_I)
     awi[...] += arc_ri[...].astype(F32)
     ars_si[...] = awi[...].astype(BF16)
 
-    def send_ars(j, _):
+    def send_ars_in(j, _):
         device, q = ar_peer(j)
         copy(ars_si.at[rows_at(q * 144, 144, 144)], ars_ri.at[rows_at((j - 1) * 144, 144, 144)], ARS_I, device).start()
-        copy(ars_so.at[rows_at(q * 16, 16, 16)], ars_ro.at[rows_at((j - 1) * 16, 16, 16)], ARS_O, device).start()
-        return 0
-
-    lax.fori_loop(1, 8, send_ars, 0)
+        return 0
+
+    lax.fori_loop(1, 8, send_ars_in, 0)
+
+    to_input(toward(UP, 4))
+    rs3_step(4)
+    rs3_step(3)
+    rs3_step(2)
+
     q = y * 2 + xl
     own_in, own_out = rows_at(q * 144, 144, 144), rows_at(q * 16, 16, 16)
     total_in, total_out = awi[own_in, :], awo[own_out, :]
+    got(ars_ro, ARS_O)
+    for j in range(7):
+        total_out = total_out + ars_ro[j * 16 : j * 16 + 16, :].astype(F32)
+    fwo[core, own_out, :] = total_out.astype(BF16)
+
+    def send_aag_out(j, _):
+        device, _ = ar_peer(j)
+        copy(fwo.at[core, own_out], fwo.at[core, own_out], AAG_O, device).start()
+        return 0
+
+    lax.fori_loop(1, 8, send_aag_out, 0)
     got(ars_ri, ARS_I)
     for j in range(7):
         total_in = total_in + ars_ri[j * 144 : j * 144 + 144, :].astype(F32)
-    got(ars_ro, ARS_O)
-    for j in range(7):
-        total_out = total_out + ars_ro[j * 16 : j * 16 + 16, :].astype(F32)
     fwi[core, own_in, :] = total_in.astype(BF16)
-    fwo[core, own_out, :] = total_out.astype(BF16)
-
-    def send_aag(j, _):
+
+    def send_aag_in(j, _):
         device, _ = ar_peer(j)
         copy(fwi.at[core, own_in], fwi.at[core, own_in], AAG_I, device).start()
-        copy(fwo.at[core, own_out], fwo.at[core, own_out], AAG_O, device).start()
-        return 0
-
-    lax.fori_loop(1, 8, send_aag, 0)
+        return 0
+
+    lax.fori_loop(1, 8, send_aag_in, 0)
+    rs3_step(1)
+    for f in (0, 1):
+        rs3xs[f * FLOW : f * FLOW + FLOW, :] = reduce_end(f, 4, mp_row, part, rs3r, RS3, rs3sem).astype(BF16)
+    copy(rs3xs, rs3xr, RS3X, across).start()
+    grad_image = jnp.concatenate([reduce_end(f, 4, mp_row, part, rs3r, RS3, rs3sem) for f in (2, 3)], axis=0)
+    grad_image = grad_image + grad_features
 
     got(lzr, LOSSZ)
     loss = lz_tile[...]
     for j in range(7):
         loss = loss + lzr[j * 8 : j * 8 + 8, :]
     loss_ref[...] = loss * (1.0 / PAIRS)
-    grad_image = grad_features + dot_nt(gh[own_rows, :], wi_ref[...])
-
+
+    got(fwo.at[core, pl.ds(0, 7 * 16)], AAG_O)
+    copy(fwo.at[core], fwo.at[core], AFC_O, partner).start()
     got(fwi.at[core, pl.ds(0, 7 * 144)], AAG_I)
     copy(fwi.at[core], fwi.at[core], AFC_I, partner).start()
-    got(fwo.at[core, pl.ds(0, 7 * 16)], AAG_O)
-    copy(fwo.at[core], fwo.at[core], AFC_O, partner).start()
-    got(rs3r, RS3)
-
-    def add_rs3(j, total):
-        return total + rs3r[rows_at(j * OWN, OWN, OWN), :].astype(F32)
-
-    gi_ref[...] = lax.fori_loop(0, 15, add_rs3, grad_image)
+    got(rs3xr, RS3X)
+    gi_ref[...] = grad_image + rs3xr[...].astype(F32)
+    got(fwo.at[1 - core], AFC_O)
+    for half in range(2):
+        gwo_ref[half * 128 : half * 128 + 128, :] = fwo[half]
     got(fwi.at[1 - core], AFC_I)
     for half in range(2):
         gwi_ref[:, half * 128 : half * 128 + 128] = fwi[half]
-    got(fwo.at[1 - core], AFC_O)
-    for half in range(2):
-        gwo_ref[half * 128 : half * 128 + 128, :] = fwo[half]
 
     sent(txt.at[pl.ds(0, 15 * OWN)], TEXT)
     sent(meta.at[0], META)
-    sent(rs1r, RS1)
+    sent(rs1s.at[pl.ds(0, 28 * FLOW)], RS1)
+    sent(rs1xs, RS1X)
     sent(img.at[pl.ds(0, 7 * OWN)], AG1Z)
     sent(img.at[pl.ds(0, 8 * OWN)], AG1C)
     sent(c_send, RS2C)
@@ -439,8 +530,10 @@
     sent(l1r, LOSS1)
     sent(lc_tile, LOSSC)
     sent(lzr, LOSSZ)
-    sent(gfall.at[pl.ds(0, 15 * OWN)], AG2)
-    sent(rs3r, RS3)
+    sent(gfall.at[pl.ds(0, 28 * FLOW)], AG2)
+    sent(rs3xs, AG2X)
+    sent(rs3s.at[pl.ds(0, 28 * FLOW)], RS3)
+    sent(rs3xs, RS3X)
     sent(arc_si, ARC_I)
     sent(arc_so, ARC_O)
     sent(ars_ri, ARS_I)
@@ -460,10 +553,21 @@
         return pltpu.VMEM(shape, kind)
 
     scratch = [
+        buf((ROWS, D)),
+        buf((OWN, D)),
+        buf((D, HID)),
+        buf((HID, D)),
+        buf((1, ROWS), jnp.int32),
+        buf((1, OWN), jnp.int32),
+        buf((1, ROWS), jnp.int32),
+        buf((8, 8), F32),
         buf((ROWS, HID), F32),
         buf((ROWS, HID)),
-        buf((ROWS, D)),
-        buf((15 * OWN, D)),
+        buf((ROWS, D), F32),
+        buf((ROWS, D)),
+        buf((ROWS, D)),
+        buf((OWN, D)),
+        buf((OWN, D)),
         buf((ROWS, D + ext)),
         buf((2, 8, 256), F32),
         buf((2, ext, 256)),
@@ -486,7 +590,9 @@
         buf((ROWS, D)),
         buf((ROWS, HID)),
         buf((ROWS, D)),
-        buf((15 * OWN, D)),
+        buf((ROWS, D)),
+        buf((OWN, D)),
+        buf((OWN, D)),
         buf((D, 128)),
         buf((128, D)),
         buf((D, 128)),
@@ -499,9 +605,13 @@
         buf((7 * 16, D)),
         buf((2, D, 128)),
         buf((2, 128, D)),
-        pltpu.SemaphoreType.DMA((21,)),
-        pltpu.SemaphoreType.DMA((21,)),
+        pltpu.SemaphoreType.DMA((8,)),
+        pltpu.SemaphoreType.DMA((24,)),
+        pltpu.SemaphoreType.DMA((24,)),
         pltpu.SemaphoreType.DMA((7,)),
+        pltpu.SemaphoreType.DMA((32,)),
+        pltpu.SemaphoreType.DMA((32,)),
+        pltpu.SemaphoreType.DMA((32,)),
     ]
     loss, grad_text, grad_image, grad_w_in, grad_w_out = pl.pallas_call(
         kernel,
@@ -512,7 +622,7 @@
             jax.ShapeDtypeStruct((D, HID), BF16),
             jax.ShapeDtypeStruct((HID, D), BF16),
         ),
-        in_specs=[vmem] * 8,
+        in_specs=[pl.BlockSpec(memory_space=pl.ANY)] * 8,
         out_specs=(vmem,) * 5,
         scratch_shapes=scratch,
         compiler_params=pltpu.CompilerParams(
@@ -521,7 +631,7 @@
         name="pairs_and_block",
     )(
         image_feats, text_feats, w_in, w_out, image_bucket[None, :], text_bucket[None, :], positive[None, :],
-        reward_table.T,
+        reward_table,
     )
     return (loss[0, 0], grad_text, grad_image, grad_w_in.astype(F32), grad_w_out.astype(F32))
 

time: 154 us -> 125 us (0.81)
  Pallas kernels: 142 us -> 113 us
    pallas_call x1, Pallas kernels: 142 us -> 113 us  [per_device(): pl.pallas_call(kernel, out_shape=(jax.ShapeDtypeStruct((8, 128), F32), ja...]
    unnamed x17 -> x18, local copies, waits for them, and re-layouts: 8.38 us -> 8.3 us
where the time goes in v2:
time: 125 us; the launch traced here: 124 us
  Pallas kernels  113 us (90%)
  local copies, waits for them, and re-layouts  8.81 us (7%)
  other arithmetic  2.19 us (2%)
    pallas_call x1, Pallas kernels, per_device(): pl.pallas_call(kernel, out_shape=(jax.ShapeDtypeStruct((8, 128), F32), ja...  113 us
    unnamed x18, local copies, waits for them, and re-layouts  8.3 us

profile of v2, /device:TPU:1, one launch (start us, length us, event | category | flops | bytes accessed | tf_op | source)
XLA Modules:
  0.0 124.3 jit_solution(8574910486785756285)
XLA Ops:
  0.6 0.0 copy-start
  0.6 1.3 %copy-done = bf16[512,1152]{1,0:T(8,128)(2,1)S(1)} copy-done((bf16[512,1152]{1,0:T(8,128)(2,1)S(1)}, bf16[512,1152]{1,0:T(8,128)(2,1)}, u32[]{:S(2)}) %copy-start) | copy-done | bytes 1179672
  1.9 0.0 copy-start.1
  1.9 1.1 copy-done.1
  3.0 0.0 copy-start.2
  3.0 1.1 copy-done.2
  4.0 0.0 copy-start.3
  4.0 0.9 copy-done.3
  4.9 0.0 copy-start.4
  4.9 0.7 copy-done.4
  5.6 0.0 copy-start.5
  5.6 0.7 copy-done.5
  6.3 0.0 copy-start.6
  6.3 0.7 copy-done.6
  7.0 0.0 copy-start.7
  7.0 0.7 copy-done.7
  7.6 112.6 %pairs_and_block.1 = (f32[8,128]{1,0:T(8,128)S(1)}, f32[32,1152]{1,0:T(8,128)S(1)}, f32[32,1152]{1,0:T(8,128)S(1)}, bf16[1152,256]{1,0:T(8,128)(2,1)S(1)}, bf16[256,1152]{1,0:T(8,128)(2,1)S(1)}) custom-call(bf16[512,1152]{1,0:T(8,128)(2,1)S(1)} %copy-done, bf16[32,1152]{1,0:T(8,128)(2,1)S(1)} %copy-done.3, bf16[1152,256]{1,0:T(8,128)(2,1)S(1)} %copy-done.1, ...), custom_call_target="tpu_custom_call" | custom-call | tf_op jit(solution)/shard_map/pairs_and_block/pallas_call | solution.py:616
  120.2 0.5 slice.3
  120.8 1.1 convert_element_type.6
  121.9 1.1 convert_element_type.7
  123.0 0.7 copy.15
  123.6 0.7 copy.16
Async XLA Ops:
  0.6 1.3 %copy-start = (bf16[512,1152]{1,0:T(8,128)(2,1)S(1)}, bf16[512,1152]{1,0:T(8,128)(2,1)}, u32[]{:S(2)}) copy-start(bf16[512,1152]{1,0:T(8,128)(2,1)} %x_hbm.1) | copy-start | bytes 3538948
  1.9 1.1 copy-start.1
  3.0 1.1 copy-start.2
  4.0 0.9 copy-start.3
  4.9 0.7 copy-start.4
  5.6 0.7 copy-start.5
  6.3 0.7 copy-start.6
  7.0 0.7 copy-start.7

commit v3 on v2

v3 whole, which is shorter than its diff:
```python
import jax
import jax.numpy as jnp
from jax import lax
from jax.experimental import pallas as pl
from jax.experimental.pallas import tpu as pltpu
from jax.sharding import PartitionSpec as P

MESH = pl.DeviceIdType.MESH
F32 = jnp.float32
BF16 = jnp.bfloat16

logit_scale = 4.0
logit_bias = -2.0
norm_eps = 1e-06
root_coef = 0.7978845608028654
cubic_coef = 0.044715

D = 1152
ROWS = 512
OWN = 32
HID = 256
PAIRS = 8192.0 * 8192.0
ext = 128
VMEM_LIMIT = 60 * 2**20

NT = (((1,), (1,)), ((), ()))
TN = (((0,), (0,)), ((), ()))


def dot(a, b):
    return jnp.dot(a, b, preferred_element_type=F32)


def dot_nt(a, b):
    return lax.dot_general(a, b, NT, preferred_element_type=F32)


def dot_tn(a, b):
    return lax.dot_general(a, b, TN, preferred_element_type=F32)


def gelu_tanh(v):
    return 0.5 * v * (1.0 + jnp.tanh(root_coef * (v + cubic_coef * v * v * v)))


def gelu_slope(v):
    t = jnp.tanh(root_coef * (v + cubic_coef * v * v * v))
    return 0.5 * (1.0 + t) + 0.5 * v * (1.0 - t * t) * root_coef * (1.0 + 3.0 * cubic_coef * v * v)


def row_norm(v):
    return jnp.sqrt(jnp.sum(v * v, axis=-1, keepdims=True) + norm_eps)


(TEXT, TEXT2, META, RS1, RS1B, RS1X, AG1C, RS2C, RS2Z, TG, TG2, LOSS1, LOSSC, LOSSZ, AG2, AG2X, RS3, RS3B, RS3X, ARC_I, ARC_O, ARS_I, ARS_O,
 AAG_I, AAG_O, AFC_I, AFC_O, AG1Z, RS1L, RS3L) = range(30)
FLOW = 16
UP, DOWN = 0, 1
SLOTS = ((0, UP), (4, UP), (3, UP), (3, DOWN), (2, UP), (2, DOWN), (1, UP), (1, DOWN))


def slot_at(way, far):
    return 0 if far == 0 else 1 if far == 4 else 8 - 2 * far + way


def rows_at(start, count, step):
    return pl.ds(pl.multiple_of(start, step), count)


def kernel(
    x_hbm, t_hbm, wi_hbm, wo_hbm, ib_hbm, tb_hbm, pos_hbm, tab_hbm,
    loss_ref, gt_ref, gi_ref, gwi_ref, gwo_ref,
    x_ref, t_ref, wi_ref, wo_ref, ib_ref, tb_ref, pos_ref, tab_ref,
    hp, act, part, rs1s, rs1r, rs1bs, rs1br, rs1ls, rs1lr, rs1xs, rs1xr, txt, meta, meta_s, meta_r, hot, img, coef, loss_acc, c_send, c_recv, ig, held, rs2s, rs2r, tgs, tgr, tgo, tgs2, tgr2,
    l_tile, l1r, lc_tile, lcr, lz_tile, lzr, gfall, gh, swi, swo, rs3s, rs3r, rs3bs, rs3br, rs3ls, rs3lr, rs3xs, rs3xr,
    arc_si, arc_so, arc_ri, arc_ro, awi, awo, ars_si, ars_so, ars_ri, ars_ro, fwi, fwo,
    lsem, ssem, rsem, csem, rs1sem, ag1sem, rs2sem, ag2sem, rs3sem, rs1bsem, ag2bsem, rs3bsem, aagsem,
):
    dp, mp = lax.axis_index("dp"), lax.axis_index("mp")
    core, y, xl = lax.rem(dp, 2), lax.rem(dp // 2, 4), dp // 8
    xh, z = lax.rem(mp, 2), mp // 2
    x = xh * 2 + xl
    partner = (dp + 1 - 2 * core, mp)

    across = (dp, mp + 1 - 2 * xh)

    def z_peer(j):
        return (dp, lax.rem(z + j, 8) * 2 + xh)

    def plane_dev(x2, y2):
        return ((lax.rem(x2, 2) * 4 + y2) * 2 + core, z * 2 + x2 // 2)

    def ar_peer(j):
        xl2, y2 = lax.rem(xl + lax.rem(j, 2), 2), lax.rem(y + j // 2, 4)
        return ((xl2 * 4 + y2) * 2 + core, mp), y2 * 2 + xl2

    def plane_peer(j):
        return plane_dev(lax.rem(x + lax.rem(j, 4), 4), lax.rem(y + j // 4, 4))

    def copy(src, dst, phase, device, recv=None):
        return pltpu.make_async_remote_copy(
            src_ref=src, dst_ref=dst, send_sem=ssem.at[phase],
            recv_sem=rsem.at[phase] if recv is None else recv, device_id=device, device_id_type=MESH,
        )

    def got(ref, phase):
        copy(ref, ref, phase, partner).wait_recv()

    def sent(ref, phase):
        copy(ref, ref, phase, partner).wait_send()

    def hops(f, way):
        return 4 if f % 2 == way else 3

    def neighbour(way):
        return z_peer(1 if way == UP else 7)

    def toward(way, far):
        return lax.rem(z + (far if way == UP else 8 - far), 8)

    barrier = pltpu.get_barrier_semaphore()

    def greet(j, _):
        pl.semaphore_signal(barrier, inc=1, device_id=plane_peer(j), device_id_type=MESH)
        return 0

    lax.fori_loop(1, 16, greet, 0)

    def greet_z(j, _):
        pl.semaphore_signal(barrier, inc=1, device_id=z_peer(j), device_id_type=MESH)
        return 0

    lax.fori_loop(1, 8, greet_z, 0)
    pl.semaphore_signal(barrier, inc=1, device_id=partner, device_id_type=MESH)

    loads = [
        pltpu.make_async_copy(src, dst, lsem.at[i])
        for i, (src, dst) in enumerate(
            (
                (t_hbm, t_ref), (tb_hbm, tb_ref), (pos_hbm, pos_ref), (ib_hbm, ib_ref), (tab_hbm, tab_ref),
                (wi_hbm, wi_ref), (wo_hbm, wo_ref),
            )
        )
    ]
    for load in loads:
        load.start()
    for far, way in SLOTS:
        for other in (0, 1):
            from_rows = rows_at((toward(way, far) * 2 + (1 - xh if other else xh)) * OWN, OWN, OWN)
            to_rows = pl.ds(slot_at(way, far) * 64 + other * OWN, OWN)
            pltpu.make_async_copy(x_hbm.at[from_rows], x_ref.at[to_rows], lsem.at[7]).start()
    for load in loads[:5]:
        load.wait()

    own_slot = y * 4 + x
    own_text = rows_at(own_slot * OWN, OWN, OWN)
    wide = t_ref[...].astype(F32)
    txt[own_text, :D] = (wide / row_norm(wide)).astype(BF16)
    eye = lax.broadcasted_iota(jnp.int32, (OWN, OWN), 0) == lax.broadcasted_iota(jnp.int32, (OWN, OWN), 1)
    tb_col = jnp.sum(jnp.where(eye, tb_ref[...].astype(F32), 0.0), axis=1, keepdims=True)
    lane = lax.broadcasted_iota(jnp.int32, (OWN, ext), 1)
    level = jnp.where(lane < 24, lax.rem(lane, 8), -1).astype(F32)
    txt[own_text, D:] = jnp.where(level == tb_col, 1.0, 0.0).astype(BF16)

    pl.semaphore_wait(barrier, 23)

    def send_text(j, _):
        device = plane_dev(lax.rem(x + j, 4), y)
        copy(txt.at[own_text], txt.at[own_text], TEXT, device).start()
        return 0

    lax.fori_loop(1, 4, send_text, 0)

    def text_on():
        got(txt.at[pl.ds(0, 3 * OWN)], TEXT)
        rows = rows_at(y * 128, 128, 128)

        def send(j, _):
            copy(txt.at[rows], txt.at[rows], TEXT2, plane_dev(x, lax.rem(y + j, 4))).start()
            return 0

        lax.fori_loop(1, 4, send, 0)

    def slot_of(f, way, far, flows):
        return pl.ds(((way * flows + f) * 4 + far - 1) * FLOW, FLOW)

    def sem_of(sems, f, way, far, flows):
        return sems.at[(way * flows + f) * 4 + far - 1]

    def last_of(f, way, last):
        return pl.ds((way + 2 * last[3].index(f)) * FLOW, FLOW)

    def reduce_step(far, which, flows, row_of, held, sbuf, rbuf, phase, sems, last):
        for f in which:
            for way in (UP, DOWN):
                if far > hops(f, way):
                    continue
                value = held[pl.ds(row_of(f, slot_at(way, far)), FLOW), :]
                if far < hops(f, way):
                    before = slot_of(f, way, far + 1, flows)
                    copy(rbuf.at[before], rbuf.at[before], phase, partner, sem_of(sems, f, way, far + 1, flows)).wait_recv()
                    value = value + rbuf[before, :].astype(F32)
                sem = sem_of(sems, f, way, far, flows)
                if f in last[3] and far == 1:
                    sbuf1, rbuf1, phase1, _ = last
                    slot = last_of(f, way, last)
                    sbuf1[slot, :] = value
                    copy(sbuf1.at[slot], rbuf1.at[slot], phase1, neighbour(way), sem).start()
                else:
                    slot = slot_of(f, way, far, flows)
                    sbuf[slot, :] = value.astype(BF16)
                    copy(sbuf.at[slot], rbuf.at[slot], phase, neighbour(way), sem).start()

    def reduce_end(f, flows, row_of, held, rbuf, phase, sems, last):
        value = held[pl.ds(row_of(f, 0), FLOW), :]
        for way in (UP, DOWN):
            slot = slot_of(f, way, 1, flows)
            if f in last[3]:
                rbuf, phase, slot = last[1], last[2], last_of(f, way, last)
            copy(rbuf.at[slot], rbuf.at[slot], phase, partner, sem_of(sems, f, way, 1, flows)).wait_recv()
            value = value + rbuf[slot, :].astype(F32)
        return value

    def gather_step(far, which, flows, row_of, buf, phase, sems):
        for f in which:
            for way in (UP, DOWN):
                if far > hops(f, way):
                    continue
                rows = pl.ds(row_of(f, slot_at(1 - way, far)), FLOW)
                if far > 0:
                    copy(buf.at[rows], buf.at[rows], phase, partner, sem_of(sems, f, way, far, flows)).wait_recv()
                if far < hops(f, way):
                    onto = pl.ds(row_of(f, slot_at(1 - way, far + 1)), FLOW)
                    copy(buf.at[rows], buf.at[onto], phase, neighbour(way), sem_of(sems, f, way, far + 1, flows)).start()

    def mp_row(f, slot):
        return slot * 64 + (OWN, 0, FLOW)[f]

    def reduce_mp(held, sbuf, rbuf, bs, br, xs, xr, last, phases, sems, bsems):
        ring_phase, b_phase, x_phase = phases

        def send_across(slots):
            for slot in slots:
                rows = pl.ds(slot * FLOW, FLOW)
                bs[rows, :] = held[slot * 64 + 48 : slot * 64 + 64, :].astype(BF16)
                copy(bs.at[rows], br.at[rows], b_phase, across, bsems.at[slot]).start()

        def ring(far):
            reduce_step(far, (0, 1), 3, mp_row, held, sbuf, rbuf, ring_phase, sems, last)

        def met(slots):
            for slot in slots:
                rows = pl.ds(slot * FLOW, FLOW)
                copy(br.at[rows], br.at[rows], b_phase, partner, bsems.at[slot]).wait_recv()
                held[slot * 64 + FLOW : slot * 64 + 2 * FLOW, :] += br[rows, :].astype(F32)

        def cross(far):
            met((1,) if far == 4 else (slot_at(UP, far), slot_at(DOWN, far)))
            reduce_step(far, (2,), 3, mp_row, held, sbuf, rbuf, ring_phase, sems, last)

        def end_across():
            xs[...] = reduce_end(0, 3, mp_row, held, rbuf, ring_phase, sems, last)
            copy(xs, xr, x_phase, across).start()
            met((0,))

        def end():
            near = reduce_end(1, 3, mp_row, held, rbuf, ring_phase, sems, last)
            mixed = reduce_end(2, 3, mp_row, held, rbuf, ring_phase, sems, last)
            got(xr, x_phase)
            return jnp.concatenate([near + xr[...], mixed], axis=0)

        return send_across, ring, cross, end_across, end

    for load in loads[5:]:
        load.wait()

    pltpu.make_async_copy(x_ref, x_ref, lsem.at[7]).wait()

    def forward(g):
        rows = pl.ds(g * 128, 128)
        pre = dot(x_ref[rows, :], wi_ref[...])
        hp[rows, :] = pre
        a = gelu_tanh(pre).astype(BF16)
        act[rows, :] = a
        part[rows, :] = dot(a, wo_ref[...])

    rs1_across, rs1_ring, rs1_cross, rs1_end_across, rs1_end = reduce_mp(
        part, rs1s, rs1r, rs1bs, rs1br, rs1xs, rs1xr, (rs1ls, rs1lr, RS1L, (2,)), (RS1, RS1B, RS1X), rs1sem, rs1bsem
    )
    forward(0)
    rs1_across((1, 0))
    rs1_ring(4)
    forward(1)
    rs1_across((2, 3))
    rs1_ring(3)
    forward(2)
    rs1_across((4, 5))
    rs1_cross(4)
    rs1_ring(2)
    forward(3)
    rs1_across((6, 7))
    rs1_cross(3)
    rs1_ring(1)
    text_on()
    pos = pos_ref[...]
    pos_hi = pos // 64
    line = lax.broadcasted_iota(jnp.int32, (8, ROWS), 0)
    table_rows = jnp.where(
        line == 0, pos_hi, jnp.where(line == 1, pos - pos_hi * 64, jnp.where(line == 2, ib_ref[...], 0))
    ).astype(F32).astype(BF16)
    took = lax.broadcasted_iota(jnp.int32, (ROWS, ROWS), 0)
    into = lax.broadcasted_iota(jnp.int32, (ROWS, ROWS), 1)
    slot = into // 64
    distance = jnp.where(lax.rem(slot, 2) == 0, 4 - slot // 2, slot // 2 + 4)
    distance = jnp.where(slot == 0, 0, jnp.where(slot == 1, 4, distance))
    right = took == (lax.rem(z + distance, 8) * 2 + xh) * OWN + lax.rem(into, OWN)
    first = lax.rem(into, 64) < OWN
    meta[...] = dot(table_rows, jnp.where(right & first, 1.0, 0.0).astype(BF16))
    meta_s[...] = dot(table_rows, jnp.where(right & jnp.logical_not(first), 1.0, 0.0).astype(BF16))

    copy(meta_s, meta_r, META, partner).start()
    rs1_cross(2)
    rs1_end_across()
    rs1_cross(1)
    features = rs1_end() + x_ref[:OWN, :].astype(F32)
    norm = row_norm(features)
    unit = features / norm

    img[:OWN, :] = unit.astype(BF16)
    def send_img(from_row, to_row, count, sem, distance):
        copy(
            img.at[pl.ds(from_row, count)], img.at[pl.ds(to_row, count)], AG1Z, z_peer(distance % 8), ag1sem.at[sem]
        ).start()

    def got_img(count, sem):
        copy(img.at[pl.ds(0, count)], img.at[pl.ds(0, count)], AG1Z, partner, ag1sem.at[sem]).wait_recv()

    for way, sign in ((UP, 1), (DOWN, -1)):
        send_img(0, slot_at(1 - way, 2) * 64, OWN, way, 2 * sign)
    for way, sign in ((UP, 1), (DOWN, -1)):
        send_img(0, slot_at(1 - way, 1) * 64, OWN, 2 + way, sign)

    def to_partner(slot):
        copy(
            img.at[pl.ds(slot * 64, OWN)], img.at[pl.ds(slot * 64 + OWN, OWN)], AG1C, partner, csem.at[slot // 2 + (4 if slot == 1 else 0)]
        ).start()

    def from_partner(far):
        count = OWN if far in (0, 4) else 2 * OWN
        copy(
            img.at[pl.ds(0, count)], img.at[pl.ds(0, count)], AG1C, partner, csem.at[0 if far == 0 else 4 - far if far < 4 else 4]
        ).wait_recv()

    to_partner(0)

    got(meta_r, META)
    meta[...] += meta_r[...]

    eye8 = lax.broadcasted_iota(jnp.int32, (8, 8), 0) == lax.broadcasted_iota(jnp.int32, (8, 8), 1)

    buckets = meta[2:3, :]
    weights = jnp.zeros((8, ROWS), F32)
    for k in range(8):
        column = jnp.sum(jnp.where(eye8, tab_ref[k : k + 1, :], 0.0), axis=1, keepdims=True)
        weights = weights + jnp.where(buckets == float(k), column, 0.0)
    hi = weights.astype(BF16).astype(F32)
    mid = (weights - hi).astype(BF16).astype(F32)
    low = weights - hi - mid
    hot[...] = jnp.concatenate([hi, mid, low, jnp.zeros((ext - 24, ROWS), F32)], axis=0).astype(BF16)
    meta[0:1, :] = meta[0:1, :] * 64.0 + meta[1:2, :]
    got(txt.at[pl.ds(0, 3 * 128)], TEXT2)

    loss_acc[...] = jnp.zeros_like(loss_acc)

    def pairs(g):
        images = pl.ds(g * 128, 128)

        logits = logit_scale * dot_nt(txt[:, :D], img[images, :]) + logit_bias
        weight = dot(txt[:, D:], hot[:, images])
        slot = lax.broadcasted_iota(jnp.int32, (ROWS, 1), 0)
        p = slot // OWN
        px, py = lax.rem(p, 4), p // 4
        index = (((lax.rem(px, 2) * 4 + py) * 2 + core) * 16 + z * 2 + px // 2) * OWN + lax.rem(slot, OWN)
        hit = index.astype(F32) == meta[0:1, images]
        against = jnp.where(hit, -logits, logits)
        grown = jnp.exp(against)
        loss_acc[...] += jnp.sum((weight * jnp.log(1.0 + grown)).reshape(ROWS // 8, 8, 128), axis=0)
        slope = logit_scale * weight * (grown / (1.0 + grown))
        coef[:, images] = jnp.where(hit, -slope, slope).astype(BF16)

    for way in (UP, DOWN):
        got_img(OWN, 2 + way)
        to_partner(slot_at(1 - way, 1))
    for way, sign in ((UP, 1), (DOWN, -1)):
        got_img(OWN, way)
        row = slot_at(1 - way, 2) * 64
        send_img(row, slot_at(1 - way, 3) * 64, OWN, 4 + way, sign)
        send_img(row + FLOW * way, 64 + FLOW * way, FLOW, 6 + way, 2 * sign)
    for way in (UP, DOWN):
        to_partner(slot_at(1 - way, 2))
    from_partner(1)
    pairs(3)
    for way in (UP, DOWN):
        got_img(OWN, 4 + way)
        to_partner(slot_at(1 - way, 3))
    from_partner(2)
    pairs(2)
    for way in (UP, DOWN):
        got_img(FLOW, 6 + way)
    to_partner(1)
    from_partner(3)
    pairs(1)
    from_partner(0)
    from_partner(4)
    pairs(0)

    def image_grad(g):
        rows = pl.ds(g * 128, 128)
        ig[rows, :] = dot_tn(coef[:, rows], txt[:, :D])
        to = pl.ds(g * 64, 64)
        for slot in (2 * g, 2 * g + 1):
            c_send[slot * OWN : slot * OWN + OWN, :] = ig[slot * 64 + OWN : slot * 64 + 64, :]
        copy(c_send.at[to], c_recv.at[to], RS2C, partner, csem.at[5 + g]).start()

    def both_cores(g):
        to = pl.ds(g * 64, 64)
        copy(c_send.at[to], c_recv.at[to], RS2C, partner, csem.at[5 + g]).wait_recv()
        for slot in (2 * g, 2 * g + 1):
            rows = pl.ds(slot * OWN, OWN)
            held[rows, :] = ig[slot * 64 : slot * 64 + OWN, :] + c_recv[rows, :]

    def send_rs2(value, sem, distance):
        rows = pl.ds(sem * OWN, value.shape[0])
        rs2s[rows, :] = value.astype(BF16)
        copy(rs2s.at[rows], rs2r.at[rows], RS2Z, z_peer(distance % 8), rs2sem.at[sem]).start()

    def got_rs2(sem, count=OWN):
        rows = pl.ds(sem * OWN, count)
        copy(rs2r.at[rows], rs2r.at[rows], RS2Z, partner, rs2sem.at[sem]).wait_recv()
        return rs2r[rows, :].astype(F32)

    def held_at(way, far):
        row = slot_at(way, far) * OWN
        return held[row : row + OWN, :]

    image_grad(0)
    image_grad(1)
    both_cores(0)
    far4 = held_at(UP, 4)
    send_rs2(far4[:FLOW], 0, 2)
    send_rs2(far4[FLOW:], 1, -2)
    image_grad(2)
    both_cores(1)
    send_rs2(held_at(UP, 3), 2, 1)
    send_rs2(held_at(DOWN, 3), 3, -1)
    image_grad(3)
    both_cores(2)
    both_cores(3)
    send_rs2(held_at(UP, 1), 6, 1)
    send_rs2(held_at(DOWN, 1), 7, -1)

    def text_grad(j, _):
        b = lax.rem(y + j, 4)
        rows = rows_at(b * 128, 128, 128)
        tgs[rows, :] = dot(coef[rows, :], img[...]).astype(BF16)
        copy(tgs.at[rows], tgr.at[rows_at((j - 1) * 128, 128, 128)], TG, plane_dev(x, b)).start()
        return 0

    lax.fori_loop(1, 3, text_grad, 0)
    far2 = held_at(UP, 2) + got_rs2(2)
    send_rs2(jnp.concatenate([far2[:FLOW] + got_rs2(0, FLOW), far2[FLOW:]], axis=0), 4, 2)
    far2 = held_at(DOWN, 2) + got_rs2(3)
    send_rs2(jnp.concatenate([far2[:FLOW], far2[FLOW:] + got_rs2(1, FLOW)], axis=0), 5, -2)
    text_grad(3, 0)
    tgo[...] = dot(coef[rows_at(y * 128, 128, 128), :], img[...])

    def text_grad_on():
        got(tgr, TG)
        tgo[...] += tgr[0:128, :].astype(F32) + tgr[128:256, :].astype(F32) + tgr[256:384, :].astype(F32)

        def send(j, _):
            x2 = lax.rem(x + j, 4)
            rows = rows_at(x2 * OWN, OWN, OWN)
            tgs2[rows, :] = tgo[rows, :].astype(BF16)
            copy(tgs2.at[rows], tgr2.at[rows_at((j - 1) * OWN, OWN, OWN)], TG2, plane_dev(x2, y)).start()
            return 0

        lax.fori_loop(1, 4, send, 0)

    l_tile[...] = jnp.zeros((8, 128), F32) + jnp.sum(loss_acc[...])

    def send_loss(j, _):
        copy(l_tile, l1r.at[rows_at((j - 1) * 8, 8, 8)], LOSS1, plane_peer(j)).start()
        return 0

    lax.fori_loop(1, 16, send_loss, 0)

    own_grad = held[0:OWN, :] + got_rs2(6) + got_rs2(7) + got_rs2(4) + got_rs2(5)
    projected = jnp.sum(unit * own_grad, axis=-1, keepdims=True)
    grad_features = (own_grad - unit * projected) / norm
    gfall[:OWN, :] = grad_features.astype(BF16)
    def cross_gf(slot):
        copy(
            gfall.at[pl.ds(slot * 64 + FLOW, FLOW)], gfall.at[pl.ds(slot * 64 + 48, FLOW)], AG2X, across, ag2bsem.at[slot]
        ).start()

    def crossed_gf(slots):
        for slot in slots:
            rows = pl.ds(slot * 64 + 48, FLOW)
            copy(gfall.at[rows], gfall.at[rows], AG2X, partner, ag2bsem.at[slot]).wait_recv()

    def ag2_step(far, which):
        gather_step(far, which, 3, mp_row, gfall, AG2, ag2sem)

    def near_step(far):
        ag2_step(far, (2, 1))
        for slot in (1,) if far == 4 else (slot_at(UP, far), slot_at(DOWN, far)):
            cross_gf(slot)

    other_rows = pl.ds(OWN, FLOW)
    copy(gfall.at[pl.ds(0, FLOW)], gfall.at[other_rows], AG2X, across).start()
    ag2_step(0, (2, 1))
    cross_gf(0)
    near_step(1)
    got(gfall.at[other_rows], AG2X)
    ag2_step(0, (0,))
    near_step(2)

    def backward(g):
        rows = pl.ds(g * 128, 128)
        gh[rows, :] = (dot_nt(gfall[rows, :], wo_ref[...]) * gelu_slope(hp[rows, :])).astype(BF16)

    def to_input(g):
        rows = pl.ds(g * 128, 128)
        part[rows, :] = dot_nt(gh[rows, :], wi_ref[...])

    rs3_across, rs3_ring, rs3_cross, rs3_end_across, rs3_end = reduce_mp(
        part, rs3s, rs3r, rs3bs, rs3br, rs3xs, rs3xr, (rs3ls, rs3lr, RS3L, (0, 1, 2)), (RS3, RS3B, RS3X), rs3sem, rs3bsem
    )

    other_cols, own_cols = rows_at((1 - core) * 128, 128, 128), rows_at(core * 128, 128, 128)
    late, early = pl.ds(0, 256), pl.ds(256, 256)

    def w_in_half(cols, out, kind):
        def step(b, _):
            some = rows_at(b * 128, 128, 128)
            out[some, :] = (swi[some, cols] + dot_tn(x_ref[late, some], gh[late, cols])).astype(kind)
            return 0

        lax.fori_loop(0, 9, step, 0)

    def w_in_early(b, _):
        some = rows_at(b * 128, 128, 128)
        swi[some, :] = dot_tn(x_ref[early, some], gh[early, :])
        return 0

    ag2_step(1, (0,))
    crossed_gf((6, 7))
    backward(3)
    near_step(3)
    ag2_step(2, (0,))
    crossed_gf((4, 5))
    backward(2)
    swo[...] = dot_tn(act[early, :], gfall[early, :])
    near_step(4)
    ag2_step(3, (0,))
    lax.fori_loop(0, 9, w_in_early, 0)
    crossed_gf((2, 3))
    backward(1)
    to_input(2)
    to_input(3)
    to_input(1)
    ag2_step(4, (0,))
    crossed_gf((0, 1))
    arc_so[...] = (swo[other_cols, :] + dot_tn(act[late, other_cols], gfall[late, :])).astype(BF16)
    copy(arc_so, arc_ro, ARC_O, partner).start()
    backward(0)
    w_in_half(other_cols, arc_si, BF16)
    copy(arc_si, arc_ri, ARC_I, partner).start()
    to_input(0)
    rs3_across((1, 2, 3))
    rs3_ring(4)
    rs3_across((4, 5, 6, 7, 0))
    awo[...] = swo[own_cols, :] + dot_tn(act[late, own_cols], gfall[late, :])
    got(arc_ro, ARC_O)
    awo[...] += arc_ro[...].astype(F32)
    ars_so[...] = awo[...].astype(BF16)

    def send_ars_out(j, _):
        device, q = ar_peer(j)
        copy(ars_so.at[rows_at(q * 16, 16, 16)], ars_ro.at[rows_at((j - 1) * 16, 16, 16)], ARS_O, device).start()
        return 0

    lax.fori_loop(1, 8, send_ars_out, 0)
    w_in_half(own_cols, awi, F32)
    got(arc_ri, ARC_I)
    awi[...] += arc_ri[...].astype(F32)
    ars_si[...] = awi[...].astype(BF16)

    def send_ars_in(j, _):
        device, q = ar_peer(j)
        copy(ars_si.at[rows_at(q * 144, 144, 144)], ars_ri.at[rows_at((j - 1) * 144, 144, 144)], ARS_I, device).start()
        return 0

    lax.fori_loop(1, 8, send_ars_in, 0)
    text_grad_on()
    rs3_ring(3)
    rs3_cross(4)
    got(l1r, LOSS1)
    loss = l_tile[...]
    for j in range(15):
        loss = loss + l1r[j * 8 : j * 8 + 8, :]
    lc_tile[...] = loss
    copy(lc_tile, lcr, LOSSC, partner).start()

    rs3_ring(2)
    rs3_cross(3)
    got(lcr, LOSSC)
    lz_tile[...] = loss + lcr[...]

    def send_loss_z(j, _):
        copy(lz_tile, lzr.at[rows_at((j - 1) * 8, 8, 8)], LOSSZ, z_peer(j)).start()
        return 0

    lax.fori_loop(1, 8, send_loss_z, 0)
    rs3_ring(1)
    rs3_cross(2)

    q = y * 2 + xl
    own_in, own_out = rows_at(q * 144, 144, 144), rows_at(q * 16, 16, 16)
    total_in, total_out = awi[own_in, :], awo[own_out, :]
    got(ars_ro, ARS_O)
    for j in range(7):
        total_out = total_out + ars_ro[j * 16 : j * 16 + 16, :].astype(F32)
    fwo[core, own_out, :] = total_out.astype(BF16)

    def send_aag_out(j, _):
        device, _ = ar_peer(j)
        copy(fwo.at[core, own_out], fwo.at[core, own_out], AAG_O, device, aagsem.at[7 + j]).start()
        return 0

    lax.fori_loop(1, 8, send_aag_out, 0)
    copy(fwo.at[core, own_out], fwo.at[core, own_out], AFC_O, partner).start()
    got(ars_ri, ARS_I)
    for j in range(7):
        total_in = total_in + ars_ri[j * 144 : j * 144 + 144, :].astype(F32)
    fwi[core, own_in, :] = total_in.astype(BF16)

    def send_aag_in(j, _):
        device, _ = ar_peer(j)
        copy(fwi.at[core, own_in], fwi.at[core, own_in], AAG_I, device, aagsem.at[j - 1]).start()
        return 0

    lax.fori_loop(1, 8, send_aag_in, 0)
    copy(fwi.at[core, own_in], fwi.at[core, own_in], AFC_I, partner).start()
    rs3_end_across()
    rs3_cross(1)
    grad_image = rs3_end() + grad_features

    got(tgr2, TG2)
    grad_text = tgo[rows_at(x * OWN, OWN, OWN), :]
    for j in range(3):
        grad_text = grad_text + tgr2[j * OWN : j * OWN + OWN, :].astype(F32)
    gt_ref[...] = grad_text
    got(lzr, LOSSZ)
    loss = lz_tile[...]
    for j in range(7):
        loss = loss + lzr[j * 8 : j * 8 + 8, :]
    loss_ref[...] = loss * (1.0 / PAIRS)

    def weights_on(j, _):
        xl2, y2 = lax.rem(xl + lax.rem(j, 2), 2), lax.rem(y + 4 - j // 2, 4)
        q2 = y2 * 2 + xl2
        out, into = rows_at(q2 * 16, 16, 16), rows_at(q2 * 144, 144, 144)
        copy(fwo.at[core, out], fwo.at[core, out], AAG_O, partner, aagsem.at[7 + j]).wait_recv()
        copy(fwo.at[core, out], fwo.at[core, out], AFC_O, partner).start()
        copy(fwi.at[core, into], fwi.at[core, into], AAG_I, partner, aagsem.at[j - 1]).wait_recv()
        copy(fwi.at[core, into], fwi.at[core, into], AFC_I, partner).start()
        return 0

    lax.fori_loop(1, 8, weights_on, 0)
    gi_ref[...] = grad_image
    got(fwo.at[1 - core], AFC_O)
    for half in range(2):
        gwo_ref[half * 128 : half * 128 + 128, :] = fwo[half]
    got(fwi.at[1 - core], AFC_I)
    for half in range(2):
        gwi_ref[:, half * 128 : half * 128 + 128] = fwi[half]

    sent(txt.at[pl.ds(0, 3 * OWN)], TEXT)
    sent(txt.at[pl.ds(0, 3 * 128)], TEXT2)
    sent(meta_s, META)
    sent(rs1s.at[pl.ds(0, 19 * FLOW)], RS1)
    sent(rs1bs, RS1B)
    sent(rs1ls, RS1L)
    sent(rs1xs, RS1X)
    sent(img.at[pl.ds(0, 14 * FLOW)], AG1Z)
    sent(img.at[pl.ds(0, 8 * OWN)], AG1C)
    sent(c_send, RS2C)
    sent(rs2s.at[pl.ds(0, 14 * FLOW)], RS2Z)
    sent(tgr, TG)
    sent(tgr2, TG2)
    sent(l1r, LOSS1)
    sent(lc_tile, LOSSC)
    sent(lzr, LOSSZ)
    sent(gfall.at[pl.ds(0, 21 * FLOW)], AG2)
    sent(gfall.at[pl.ds(0, 9 * FLOW)], AG2X)
    sent(rs3s.at[pl.ds(0, 15 * FLOW)], RS3)
    sent(rs3bs, RS3B)
    sent(rs3ls, RS3L)
    sent(rs3xs, RS3X)
    sent(arc_si, ARC_I)
    sent(arc_so, ARC_O)
    sent(ars_ri, ARS_I)
    sent(ars_ro, ARS_O)
    sent(fwi.at[0, pl.ds(0, 7 * 144)], AAG_I)
    sent(fwo.at[0, pl.ds(0, 7 * 16)], AAG_O)
    sent(fwi.at[0], AFC_I)
    sent(fwo.at[0], AFC_O)


def widen(loss_in, gt_in, gi_in, gwi_in, gwo_in, loss_ref, gt_ref, gi_ref, gwi_ref, gwo_ref):
    loss_ref[0, 0] = jnp.max(loss_in[...])
    gt_ref[...] = gt_in[...]
    gi_ref[...] = gi_in[...]
    gwi_ref[...] = gwi_in[...].astype(F32)
    gwo_ref[...] = gwo_in[...].astype(F32)


def per_device(
    image_feats, text_feats, w_in, w_out, image_bucket, text_bucket, positive, reward_table
):
    vmem = pl.BlockSpec(memory_space=pltpu.VMEM)

    def buf(shape, kind=BF16):
        return pltpu.VMEM(shape, kind)

    scratch = [
        buf((ROWS, D)),
        buf((OWN, D)),
        buf((D, HID)),
        buf((HID, D)),
        buf((1, ROWS), jnp.int32),
        buf((1, OWN), jnp.int32),
        buf((1, ROWS), jnp.int32),
        buf((8, 8), F32),
        buf((ROWS, HID), F32),
        buf((ROWS, HID)),
        buf((ROWS, D), F32),
        buf((ROWS, D)),
        buf((ROWS, D)),
        buf((8 * FLOW, D)),
        buf((8 * FLOW, D)),
        buf((2 * FLOW, D), F32),
        buf((2 * FLOW, D), F32),
        buf((FLOW, D), F32),
        buf((FLOW, D), F32),
        buf((ROWS, D + ext)),
        buf((8, ROWS), F32),
        buf((8, ROWS), F32),
        buf((8, ROWS), F32),
        buf((ext, ROWS)),
        buf((ROWS, D)),
        buf((ROWS, ROWS)),
        buf((8, 128), F32),
        buf((256, D), F32),
        buf((256, D), F32),
        buf((ROWS, D), F32),
        buf((256, D), F32),
        buf((256, D)),
        buf((256, D)),
        buf((ROWS, D)),
        buf((3 * 128, D)),
        buf((128, D), F32),
        buf((128, D)),
        buf((3 * OWN, D)),
        buf((8, 128), F32),
        buf((15 * 8, 128), F32),
        buf((8, 128), F32),
        buf((8, 128), F32),
        buf((8, 128), F32),
        buf((7 * 8, 128), F32),
        buf((ROWS, D)),
        buf((ROWS, HID)),
        buf((D, HID), F32),
        buf((HID, D), F32),
        buf((ROWS, D)),
        buf((ROWS, D)),
        buf((8 * FLOW, D)),
        buf((8 * FLOW, D)),
        buf((6 * FLOW, D), F32),
        buf((6 * FLOW, D), F32),
        buf((FLOW, D), F32),
        buf((FLOW, D), F32),
        buf((D, 128)),
        buf((128, D)),
        buf((D, 128)),
        buf((128, D)),
        buf((D, 128), F32),
        buf((128, D), F32),
        buf((D, 128)),
        buf((128, D)),
        buf((7 * 144, 128)),
        buf((7 * 16, D)),
        buf((2, D, 128)),
        buf((2, 128, D)),
        pltpu.SemaphoreType.DMA((8,)),
        pltpu.SemaphoreType.DMA((30,)),
        pltpu.SemaphoreType.DMA((30,)),
        pltpu.SemaphoreType.DMA((9,)),
        pltpu.SemaphoreType.DMA((24,)),
        pltpu.SemaphoreType.DMA((8,)),
        pltpu.SemaphoreType.DMA((8,)),
        pltpu.SemaphoreType.DMA((24,)),
        pltpu.SemaphoreType.DMA((24,)),
        pltpu.SemaphoreType.DMA((8,)),
        pltpu.SemaphoreType.DMA((8,)),
        pltpu.SemaphoreType.DMA((8,)),
        pltpu.SemaphoreType.DMA((15,)),
    ]
    partial = pl.pallas_call(
        kernel,
        out_shape=(
            jax.ShapeDtypeStruct((8, 128), F32),
            jax.ShapeDtypeStruct((OWN, D), F32),
            jax.ShapeDtypeStruct((OWN, D), F32),
            jax.ShapeDtypeStruct((D, HID), BF16),
            jax.ShapeDtypeStruct((HID, D), BF16),
        ),
        in_specs=[pl.BlockSpec(memory_space=pltpu.HBM)] * 8,
        out_specs=(vmem,) * 5,
        scratch_shapes=scratch,
        compiler_params=pltpu.CompilerParams(
            collective_id=0, has_side_effects=True, vmem_limit_bytes=VMEM_LIMIT
        ),
        name="pairs_and_block",
    )(
        image_feats, text_feats, w_in, w_out, image_bucket[None, :], text_bucket[None, :], positive[None, :],
        reward_table,
    )
    loss, grad_text, grad_image, grad_w_in, grad_w_out = pl.pallas_call(
        widen,
        out_shape=(
            jax.ShapeDtypeStruct((1, 1), F32),
            jax.ShapeDtypeStruct((OWN, D), F32),
            jax.ShapeDtypeStruct((OWN, D), F32),
            jax.ShapeDtypeStruct((D, HID), F32),
            jax.ShapeDtypeStruct((HID, D), F32),
        ),
        in_specs=[vmem] * 5,
        out_specs=(pl.BlockSpec(memory_space=pltpu.SMEM),) + (vmem,) * 4,
        compiler_params=pltpu.CompilerParams(vmem_limit_bytes=VMEM_LIMIT),
        name="widen",
    )(*partial)
    return (loss.reshape(()), grad_text, grad_image, grad_w_in, grad_w_out)


def solution(mesh):
    return jax.shard_map(
        per_device,
        mesh=mesh,
        in_specs=(
            P("dp", None),
            P(("dp", "mp"), None),
            P(None, "mp"),
            P("mp", None),
            P("dp"),
            P(("dp", "mp")),
            P("dp"),
            P(),
        ),
        out_specs=(P(), P(("dp", "mp"), None), P(("dp", "mp"), None), P(None, "mp"), P("mp", None)),
        check_vma=False,
    )
```

time: 125 us -> 113 us (0.904)
  local copies, waits for them, and re-layouts: 8.81 us -> 0 us
  other arithmetic: 2.19 us -> 0 us
    unnamed x18 -> x0, local copies, waits for them, and re-layouts: 8.3 us -> none
    pallas_call x1, Pallas kernels: 113 us -> 109 us  [per_device(): pl.pallas_call(kernel, out_shape=(jax.ShapeDtypeStruct((8, 128), F32), ja...]
    pallas_call x0 -> x1, Pallas kernels: none -> 2.9 us  [per_device(): pl.pallas_call(widen, out_shape=(jax.ShapeDtypeStruct((1, 1), F32), jax.S...]
    convert_element_type x2 -> x0, other arithmetic: 2.19 us -> none  [the longest x1 1.1 us: per_device(): grad_w_in.astype(F32)]
where the time goes in v3:
time: 113 us
  Pallas kernels  112 us (99%)
    pallas_call x1, Pallas kernels, per_device(): pl.pallas_call(kernel, out_shape=(jax.ShapeDtypeStruct((8, 128), F32), ja...  109 us
    pallas_call x1, Pallas kernels, per_device(): pl.pallas_call(widen, out_shape=(jax.ShapeDtypeStruct((1, 1), F32), jax.S...  2.9 us

profile of v3, /device:TPU:1, one launch (start us, length us, event | category | flops | bytes accessed | tf_op | source)
XLA Modules:
  0.0 112.9 jit_solution(16718545638351730107)
XLA Ops:
  0.6 109.4 %pairs_and_block.1 = (f32[8,128]{1,0:T(8,128)}, f32[32,1152]{1,0:T(8,128)}, f32[32,1152]{1,0:T(8,128)}, bf16[1152,256]{1,0:T(8,128)(2,1)}, bf16[256,1152]{1,0:T(8,128)(2,1)}) custom-call(bf16[512,1152]{1,0:T(8,128)(2,1)} %x_hbm.1, bf16[32,1152]{1,0:T(8,128)(2,1)} %t_hbm.1, bf16[1152,256]{1,0:T(8,128)(2,1)} %wi_hbm.1, bf16[256,1152]{1,0:T(8,128)(2,1)} %wo_hbm.1, ...), custom_call_target="tpu_custom_call" | custom-call | tf_op jit(solution)/shard_map/pairs_and_block/pallas_call | solution.py:821
  110.0 2.9 %widen.1 = (f32[1,1]{1,0:T(1,128)}, f32[32,1152]{1,0:T(8,128)}, f32[32,1152]{1,0:T(8,128)}, f32[1152,256]{1,0:T(8,128)}, f32[256,1152]{1,0:T(8,128)}) custom-call(f32[8,128]{1,0:T(8,128)} %get-tuple-element.15.loss_in, f32[32,1152]{1,0:T(8,128)} %get-tuple-element.16.gt_in, f32[32,1152]{1,0:T(8,128)} %get-tuple-element.17.gi_in, ...), custom_call_target="tpu_custom_call" | custom-call | tf_op jit(solution)/shard_map/widen/pallas_call | solution.py:841

commit v4 on v3

--- a/solution.py
+++ b/solution.py
@@ -71,7 +71,7 @@
     x_hbm, t_hbm, wi_hbm, wo_hbm, ib_hbm, tb_hbm, pos_hbm, tab_hbm,
     loss_ref, gt_ref, gi_ref, gwi_ref, gwo_ref,
     x_ref, t_ref, wi_ref, wo_ref, ib_ref, tb_ref, pos_ref, tab_ref,
-    hp, act, part, rs1s, rs1r, rs1bs, rs1br, rs1ls, rs1lr, rs1xs, rs1xr, txt, meta, meta_s, meta_r, hot, img, coef, loss_acc, c_send, c_recv, ig, held, rs2s, rs2r, tgs, tgr, tgo, tgs2, tgr2,
+    xt, hp, act, part, rs1s, rs1r, rs1bs, rs1br, rs1ls, rs1lr, rs1xs, rs1xr, txt, meta, meta_s, meta_r, hot, img, coef, loss_acc, c_send, c_recv, ig, held, rs2s, rs2r, tgs, tgr, tgo, tgs2, tgr2,
     l_tile, l1r, lc_tile, lcr, lz_tile, lzr, gfall, gh, swi, swo, rs3s, rs3r, rs3bs, rs3br, rs3ls, rs3lr, rs3xs, rs3xr,
     arc_si, arc_so, arc_ri, arc_ro, awi, awo, ars_si, ars_so, ars_ri, ars_ro, fwi, fwo,
     lsem, ssem, rsem, csem, rs1sem, ag1sem, rs2sem, ag2sem, rs3sem, rs1bsem, ag2bsem, rs3bsem, aagsem,
@@ -112,8 +112,8 @@
     def hops(f, way):
         return 4 if f % 2 == way else 3
 
-    def neighbour(way):
-        return z_peer(1 if way == UP else 7)
+    def neighbour(way, distance=1):
+        return z_peer(distance if way == UP else 8 - distance)
 
     def toward(way, far):
         return lax.rem(z + (far if way == UP else 8 - far), 8)
@@ -196,10 +196,11 @@
                 if far > hops(f, way):
                     continue
                 value = held[pl.ds(row_of(f, slot_at(way, far)), FLOW), :]
-                if far < hops(f, way):
-                    before = slot_of(f, way, far + 1, flows)
-                    copy(rbuf.at[before], rbuf.at[before], phase, partner, sem_of(sems, f, way, far + 1, flows)).wait_recv()
-                    value = value + rbuf[before, :].astype(F32)
+                for beyond in {1: (2,), 2: (3, 4)}.get(far, ()):
+                    if beyond <= hops(f, way):
+                        before = slot_of(f, way, beyond, flows)
+                        copy(rbuf.at[before], rbuf.at[before], phase, partner, sem_of(sems, f, way, beyond, flows)).wait_recv()
+                        value = value + rbuf[before, :].astype(F32)
                 sem = sem_of(sems, f, way, far, flows)
                 if f in last[3] and far == 1:
                     sbuf1, rbuf1, phase1, _ = last
@@ -209,7 +210,7 @@
                 else:
                     slot = slot_of(f, way, far, flows)
                     sbuf[slot, :] = value.astype(BF16)
-                    copy(sbuf.at[slot], rbuf.at[slot], phase, neighbour(way), sem).start()
+                    copy(sbuf.at[slot], rbuf.at[slot], phase, neighbour(way, 2 if far == 4 else 1), sem).start()
 
     def reduce_end(f, flows, row_of, held, rbuf, phase, sems, last):
         value = held[pl.ds(row_of(f, 0), FLOW), :]
@@ -229,9 +230,11 @@
                 rows = pl.ds(row_of(f, slot_at(1 - way, far)), FLOW)
                 if far > 0:
                     copy(buf.at[rows], buf.at[rows], phase, partner, sem_of(sems, f, way, far, flows)).wait_recv()
-                if far < hops(f, way):
-                    onto = pl.ds(row_of(f, slot_at(1 - way, far + 1)), FLOW)
-                    copy(buf.at[rows], buf.at[onto], phase, neighbour(way), sem_of(sems, f, way, far + 1, flows)).start()
+                for distance in {0: (1,), 1: (1,), 2: (1, 2)}.get(far, ()):
+                    if far + distance <= hops(f, way):
+                        onto = pl.ds(row_of(f, slot_at(1 - way, far + distance)), FLOW)
+                        sem = sem_of(sems, f, way, far + distance, flows)
+                        copy(buf.at[rows], buf.at[onto], phase, neighbour(way, distance), sem).start()
 
     def mp_row(f, slot):
         return slot * 64 + (OWN, 0, FLOW)[f]
@@ -296,12 +299,14 @@
     forward(2)
     rs1_across((4, 5))
     rs1_cross(4)
+    text_on()
     rs1_ring(2)
     forward(3)
     rs1_across((6, 7))
     rs1_cross(3)
     rs1_ring(1)
-    text_on()
+    for g in range(4):
+        xt[:, g * 128 : g * 128 + 128] = x_ref[g * 128 : g * 128 + 128, :].T
     pos = pos_ref[...]
     pos_hi = pos // 64
     line = lax.broadcasted_iota(jnp.int32, (8, ROWS), 0)
@@ -542,17 +547,7 @@
     late, early = pl.ds(0, 256), pl.ds(256, 256)
 
     def w_in_half(cols, out, kind):
-        def step(b, _):
-            some = rows_at(b * 128, 128, 128)
-            out[some, :] = (swi[some, cols] + dot_tn(x_ref[late, some], gh[late, cols])).astype(kind)
-            return 0
-
-        lax.fori_loop(0, 9, step, 0)
-
-    def w_in_early(b, _):
-        some = rows_at(b * 128, 128, 128)
-        swi[some, :] = dot_tn(x_ref[early, some], gh[early, :])
-        return 0
+        out[...] = (swi[:, cols] + dot(xt[:, late], gh[late, cols])).astype(kind)
 
     ag2_step(1, (0,))
     crossed_gf((6, 7))
@@ -564,12 +559,13 @@
     swo[...] = dot_tn(act[early, :], gfall[early, :])
     near_step(4)
     ag2_step(3, (0,))
-    lax.fori_loop(0, 9, w_in_early, 0)
+    swi[...] = dot(xt[:, early], gh[early, :])
     crossed_gf((2, 3))
     backward(1)
     to_input(2)
     to_input(3)
     to_input(1)
+    text_grad_on()
     ag2_step(4, (0,))
     crossed_gf((0, 1))
     arc_so[...] = (swo[other_cols, :] + dot_tn(act[late, other_cols], gfall[late, :])).astype(BF16)
@@ -603,7 +599,6 @@
         return 0
 
     lax.fori_loop(1, 8, send_ars_in, 0)
-    text_grad_on()
     rs3_ring(3)
     rs3_cross(4)
     got(l1r, LOSS1)
@@ -744,6 +739,7 @@
         buf((1, OWN), jnp.int32),
         buf((1, ROWS), jnp.int32),
         buf((8, 8), F32),
+        buf((D, ROWS)),
         buf((ROWS, HID), F32),
         buf((ROWS, HID)),
         buf((ROWS, D), F32),

time: 113 us -> 109 us (0.965)
  Pallas kernels: 112 us -> 109 us
    pallas_call x1, Pallas kernels: 109 us -> 106 us  [per_device(): pl.pallas_call(kernel, out_shape=(jax.ShapeDtypeStruct((8, 128), F32), ja...]
where the time goes in v4:
time: 109 us
  Pallas kernels  109 us (100%)
    pallas_call x1, Pallas kernels, per_device(): pl.pallas_call(kernel, out_shape=(jax.ShapeDtypeStruct((8, 128), F32), ja...  106 us
    pallas_call x1, Pallas kernels, per_device(): pl.pallas_call(widen, out_shape=(jax.ShapeDtypeStruct((1, 1), F32), jax.S...  2.9 us

profile of v4, /device:TPU:1, one launch (start us, length us, event | category | flops | bytes accessed | tf_op | source)
XLA Modules:
  0.0 109.2 jit_solution(8182834351860930794)
XLA Ops:
  0.6 105.7 %pairs_and_block.1 = (f32[8,128]{1,0:T(8,128)}, f32[32,1152]{1,0:T(8,128)}, f32[32,1152]{1,0:T(8,128)}, bf16[1152,256]{1,0:T(8,128)(2,1)}, bf16[256,1152]{1,0:T(8,128)(2,1)}) custom-call(bf16[512,1152]{1,0:T(8,128)(2,1)} %x_hbm.1, bf16[32,1152]{1,0:T(8,128)(2,1)} %t_hbm.1, bf16[1152,256]{1,0:T(8,128)(2,1)} %wi_hbm.1, bf16[256,1152]{1,0:T(8,128)(2,1)} %wo_hbm.1, ...), custom_call_target="tpu_custom_call" | custom-call | tf_op jit(solution)/shard_map/pairs_and_block/pallas_call | solution.py:817
  106.3 2.9 %widen.1 = (f32[1,1]{1,0:T(1,128)}, f32[32,1152]{1,0:T(8,128)}, f32[32,1152]{1,0:T(8,128)}, f32[1152,256]{1,0:T(8,128)}, f32[256,1152]{1,0:T(8,128)}) custom-call(f32[8,128]{1,0:T(8,128)} %get-tuple-element.15.loss_in, f32[32,1152]{1,0:T(8,128)} %get-tuple-element.16.gt_in, f32[32,1152]{1,0:T(8,128)} %get-tuple-element.17.gi_in, ...), custom_call_target="tpu_custom_call" | custom-call | tf_op jit(solution)/shard_map/widen/pallas_call | solution.py:837

commit v5 on v4

--- a/solution.py
+++ b/solution.py
@@ -52,8 +52,8 @@
     return jnp.sqrt(jnp.sum(v * v, axis=-1, keepdims=True) + norm_eps)
 
 
-(TEXT, TEXT2, META, RS1, RS1B, RS1X, AG1C, RS2C, RS2Z, TG, TG2, LOSS1, LOSSC, LOSSZ, AG2, AG2X, RS3, RS3B, RS3X, ARC_I, ARC_O, ARS_I, ARS_O,
- AAG_I, AAG_O, AFC_I, AFC_O, AG1Z, RS1L, RS3L) = range(30)
+(TEXT, TEXT2, META, RS1, RS1B, RS1X, AG1C, RS2C, RS2Z, TG, TG2, LOSS1, LOSSC, LOSSZ, AG2, AG2X, RS3, RS3X, ARC_I, ARC_O, ARS_I, ARS_O,
+ AAG_I, AAG_O, AFC_I, AFC_O, AG1Z, RS1L) = range(28)
 FLOW = 16
 UP, DOWN = 0, 1
 SLOTS = ((0, UP), (4, UP), (3, UP), (3, DOWN), (2, UP), (2, DOWN), (1, UP), (1, DOWN))
@@ -72,9 +72,9 @@
     loss_ref, gt_ref, gi_ref, gwi_ref, gwo_ref,
     x_ref, t_ref, wi_ref, wo_ref, ib_ref, tb_ref, pos_ref, tab_ref,
     xt, hp, act, part, rs1s, rs1r, rs1bs, rs1br, rs1ls, rs1lr, rs1xs, rs1xr, txt, meta, meta_s, meta_r, hot, img, coef, loss_acc, c_send, c_recv, ig, held, rs2s, rs2r, tgs, tgr, tgo, tgs2, tgr2,
-    l_tile, l1r, lc_tile, lcr, lz_tile, lzr, gfall, gh, swi, swo, rs3s, rs3r, rs3bs, rs3br, rs3ls, rs3lr, rs3xs, rs3xr,
+    l_tile, l1r, lc_tile, lcr, lz_tile, lzr, gfall, gh, swi, swo, rs3s, rs3r, rs3xs, rs3xr,
     arc_si, arc_so, arc_ri, arc_ro, awi, awo, ars_si, ars_so, ars_ri, ars_ro, fwi, fwo,
-    lsem, ssem, rsem, csem, rs1sem, ag1sem, rs2sem, ag2sem, rs3sem, rs1bsem, ag2bsem, rs3bsem, aagsem,
+    lsem, ssem, rsem, csem, rs1sem, ag1sem, rs2sem, ag2sem, rs3sem, rs1bsem, ag2bsem, aagsem,
 ):
     dp, mp = lax.axis_index("dp"), lax.axis_index("mp")
     core, y, xl = lax.rem(dp, 2), lax.rem(dp // 2, 4), dp // 8
@@ -237,7 +237,7 @@
                         copy(buf.at[rows], buf.at[onto], phase, neighbour(way, distance), sem).start()
 
     def mp_row(f, slot):
-        return slot * 64 + (OWN, 0, FLOW)[f]
+        return slot * 64 + (OWN, 0, FLOW, OWN + FLOW)[f]
 
     def reduce_mp(held, sbuf, rbuf, bs, br, xs, xr, last, phases, sems, bsems):
         ring_phase, b_phase, x_phase = phases
@@ -539,9 +539,13 @@
         rows = pl.ds(g * 128, 128)
         part[rows, :] = dot_nt(gh[rows, :], wi_ref[...])
 
-    rs3_across, rs3_ring, rs3_cross, rs3_end_across, rs3_end = reduce_mp(
-        part, rs3s, rs3r, rs3bs, rs3br, rs3xs, rs3xr, (rs3ls, rs3lr, RS3L, (0, 1, 2)), (RS3, RS3B, RS3X), rs3sem, rs3bsem
-    )
+    rs3_last = (None, None, None, ())
+
+    def rs3_ring(far):
+        reduce_step(far, (0, 3, 1, 2), 4, mp_row, part, rs3s, rs3r, RS3, rs3sem, rs3_last)
+
+    def rs3_end(flows):
+        return jnp.concatenate([reduce_end(f, 4, mp_row, part, rs3r, RS3, rs3sem, rs3_last) for f in flows], axis=0)
 
     other_cols, own_cols = rows_at((1 - core) * 128, 128, 128), rows_at(core * 128, 128, 128)
     late, early = pl.ds(0, 256), pl.ds(256, 256)
@@ -565,7 +569,6 @@
     to_input(2)
     to_input(3)
     to_input(1)
-    text_grad_on()
     ag2_step(4, (0,))
     crossed_gf((0, 1))
     arc_so[...] = (swo[other_cols, :] + dot_tn(act[late, other_cols], gfall[late, :])).astype(BF16)
@@ -574,9 +577,8 @@
     w_in_half(other_cols, arc_si, BF16)
     copy(arc_si, arc_ri, ARC_I, partner).start()
     to_input(0)
-    rs3_across((1, 2, 3))
     rs3_ring(4)
-    rs3_across((4, 5, 6, 7, 0))
+    rs3_ring(3)
     awo[...] = swo[own_cols, :] + dot_tn(act[late, own_cols], gfall[late, :])
     got(arc_ro, ARC_O)
     awo[...] += arc_ro[...].astype(F32)
@@ -599,8 +601,8 @@
         return 0
 
     lax.fori_loop(1, 8, send_ars_in, 0)
-    rs3_ring(3)
-    rs3_cross(4)
+    text_grad_on()
+    rs3_ring(2)
     got(l1r, LOSS1)
     loss = l_tile[...]
     for j in range(15):
@@ -608,18 +610,7 @@
     lc_tile[...] = loss
     copy(lc_tile, lcr, LOSSC, partner).start()
 
-    rs3_ring(2)
-    rs3_cross(3)
-    got(lcr, LOSSC)
-    lz_tile[...] = loss + lcr[...]
-
-    def send_loss_z(j, _):
-        copy(lz_tile, lzr.at[rows_at((j - 1) * 8, 8, 8)], LOSSZ, z_peer(j)).start()
-        return 0
-
-    lax.fori_loop(1, 8, send_loss_z, 0)
     rs3_ring(1)
-    rs3_cross(2)
 
     q = y * 2 + xl
     own_in, own_out = rows_at(q * 144, 144, 144), rows_at(q * 16, 16, 16)
@@ -648,10 +639,29 @@
 
     lax.fori_loop(1, 8, send_aag_in, 0)
     copy(fwi.at[core, own_in], fwi.at[core, own_in], AFC_I, partner).start()
-    rs3_end_across()
-    rs3_cross(1)
-    grad_image = rs3_end() + grad_features
-
+    got(lcr, LOSSC)
+    lz_tile[...] = loss + lcr[...]
+
+    def send_loss_z(j, _):
+        copy(lz_tile, lzr.at[rows_at((j - 1) * 8, 8, 8)], LOSSZ, z_peer(j)).start()
+        return 0
+
+    lax.fori_loop(1, 8, send_loss_z, 0)
+    rs3xs[...] = rs3_end((0, 3))
+    copy(rs3xs, rs3xr, RS3X, across).start()
+    grad_image = rs3_end((1, 2)) + grad_features
+
+    def weights_on(j, _):
+        xl2, y2 = lax.rem(xl + lax.rem(j, 2), 2), lax.rem(y + 4 - j // 2, 4)
+        q2 = y2 * 2 + xl2
+        out, into = rows_at(q2 * 16, 16, 16), rows_at(q2 * 144, 144, 144)
+        copy(fwo.at[core, out], fwo.at[core, out], AAG_O, partner, aagsem.at[7 + j]).wait_recv()
+        copy(fwo.at[core, out], fwo.at[core, out], AFC_O, partner).start()
+        copy(fwi.at[core, into], fwi.at[core, into], AAG_I, partner, aagsem.at[j - 1]).wait_recv()
+        copy(fwi.at[core, into], fwi.at[core, into], AFC_I, partner).start()
+        return 0
+
+    lax.fori_loop(1, 8, weights_on, 0)
     got(tgr2, TG2)
     grad_text = tgo[rows_at(x * OWN, OWN, OWN), :]
     for j in range(3):
@@ -663,18 +673,8 @@
         loss = loss + lzr[j * 8 : j * 8 + 8, :]
     loss_ref[...] = loss * (1.0 / PAIRS)
 
-    def weights_on(j, _):
-        xl2, y2 = lax.rem(xl + lax.rem(j, 2), 2), lax.rem(y + 4 - j // 2, 4)
-        q2 = y2 * 2 + xl2
-        out, into = rows_at(q2 * 16, 16, 16), rows_at(q2 * 144, 144, 144)
-        copy(fwo.at[core, out], fwo.at[core, out], AAG_O, partner, aagsem.at[7 + j]).wait_recv()
-        copy(fwo.at[core, out], fwo.at[core, out], AFC_O, partner).start()
-        copy(fwi.at[core, into], fwi.at[core, into], AAG_I, partner, aagsem.at[j - 1]).wait_recv()
-        copy(fwi.at[core, into], fwi.at[core, into], AFC_I, partner).start()
-        return 0
-
-    lax.fori_loop(1, 8, weights_on, 0)
-    gi_ref[...] = grad_image
+    got(rs3xr, RS3X)
+    gi_ref[...] = grad_image + rs3xr[...]
     got(fwo.at[1 - core], AFC_O)
     for half in range(2):
         gwo_ref[half * 128 : half * 128 + 128, :] = fwo[half]
@@ -700,9 +700,7 @@
     sent(lzr, LOSSZ)
     sent(gfall.at[pl.ds(0, 21 * FLOW)], AG2)
     sent(gfall.at[pl.ds(0, 9 * FLOW)], AG2X)
-    sent(rs3s.at[pl.ds(0, 15 * FLOW)], RS3)
-    sent(rs3bs, RS3B)
-    sent(rs3ls, RS3L)
+    sent(rs3s.at[pl.ds(0, 28 * FLOW)], RS3)
     sent(rs3xs, RS3X)
     sent(arc_si, ARC_I)
     sent(arc_so, ARC_O)
@@ -782,12 +780,8 @@
         buf((HID, D), F32),
         buf((ROWS, D)),
         buf((ROWS, D)),
-        buf((8 * FLOW, D)),
-        buf((8 * FLOW, D)),
-        buf((6 * FLOW, D), F32),
-        buf((6 * FLOW, D), F32),
-        buf((FLOW, D), F32),
-        buf((FLOW, D), F32),
+        buf((OWN, D), F32),
+        buf((OWN, D), F32),
         buf((D, 128)),
         buf((128, D)),
         buf((D, 128)),
@@ -801,15 +795,14 @@
         buf((2, D, 128)),
         buf((2, 128, D)),
         pltpu.SemaphoreType.DMA((8,)),
-        pltpu.SemaphoreType.DMA((30,)),
-        pltpu.SemaphoreType.DMA((30,)),
+        pltpu.SemaphoreType.DMA((28,)),
+        pltpu.SemaphoreType.DMA((28,)),
         pltpu.SemaphoreType.DMA((9,)),
         pltpu.SemaphoreType.DMA((24,)),
         pltpu.SemaphoreType.DMA((8,)),
         pltpu.SemaphoreType.DMA((8,)),
         pltpu.SemaphoreType.DMA((24,)),
-        pltpu.SemaphoreType.DMA((24,)),
-        pltpu.SemaphoreType.DMA((8,)),
+        pltpu.SemaphoreType.DMA((32,)),
         pltpu.SemaphoreType.DMA((8,)),
         pltpu.SemaphoreType.DMA((8,)),
         pltpu.SemaphoreType.DMA((15,)),

time: 109 us -> 107 us (0.982)
  Pallas kernels: 109 us -> 107 us
    pallas_call x1, Pallas kernels: 106 us -> 104 us  [per_device(): pl.pallas_call(kernel, out_shape=(jax.ShapeDtypeStruct((8, 128), F32), ja...]
where the time goes in v5:
time: 107 us
  Pallas kernels  107 us (100%)
    pallas_call x1, Pallas kernels, per_device(): pl.pallas_call(kernel, out_shape=(jax.ShapeDtypeStruct((8, 128), F32), ja...  104 us
    pallas_call x1, Pallas kernels, per_device(): pl.pallas_call(widen, out_shape=(jax.ShapeDtypeStruct((1, 1), F32), jax.S...  2.9 us

profile of v5, /device:TPU:1, one launch (start us, length us, event | category | flops | bytes accessed | tf_op | source)
XLA Modules:
  0.0 107.2 jit_solution(10885128339870959402)
XLA Ops:
  0.6 103.6 %pairs_and_block.1 = (f32[8,128]{1,0:T(8,128)}, f32[32,1152]{1,0:T(8,128)}, f32[32,1152]{1,0:T(8,128)}, bf16[1152,256]{1,0:T(8,128)(2,1)}, bf16[256,1152]{1,0:T(8,128)(2,1)}) custom-call(bf16[512,1152]{1,0:T(8,128)(2,1)} %x_hbm.1, bf16[32,1152]{1,0:T(8,128)(2,1)} %t_hbm.1, bf16[1152,256]{1,0:T(8,128)(2,1)} %wi_hbm.1, bf16[256,1152]{1,0:T(8,128)(2,1)} %wo_hbm.1, ...), custom_call_target="tpu_custom_call" | custom-call | tf_op jit(solution)/shard_map/pairs_and_block/pallas_call | solution.py:810
  104.3 2.9 %widen.1 = (f32[1,1]{1,0:T(1,128)}, f32[32,1152]{1,0:T(8,128)}, f32[32,1152]{1,0:T(8,128)}, f32[1152,256]{1,0:T(8,128)}, f32[256,1152]{1,0:T(8,128)}) custom-call(f32[8,128]{1,0:T(8,128)} %get-tuple-element.15.loss_in, f32[32,1152]{1,0:T(8,128)} %get-tuple-element.16.gt_in, f32[32,1152]{1,0:T(8,128)} %get-tuple-element.17.gi_in, ...), custom_call_target="tpu_custom_call" | custom-call | tf_op jit(solution)/shard_map/widen/pallas_call | solution.py:830

commit v6 on v5

--- a/solution.py
+++ b/solution.py
@@ -56,6 +56,7 @@
  AAG_I, AAG_O, AFC_I, AFC_O, AG1Z, RS1L) = range(28)
 FLOW = 16
 UP, DOWN = 0, 1
+FAR_FIRST = (5, 4, 7, 3, 6, 2, 1)
 SLOTS = ((0, UP), (4, UP), (3, UP), (3, DOWN), (2, UP), (2, DOWN), (1, UP), (1, DOWN))
 
 
@@ -164,22 +165,24 @@
 
     pl.semaphore_wait(barrier, 23)
 
-    def send_text(j, _):
-        device = plane_dev(lax.rem(x + j, 4), y)
-        copy(txt.at[own_text], txt.at[own_text], TEXT, device).start()
-        return 0
-
-    lax.fori_loop(1, 4, send_text, 0)
+    def send_text_y(slot_x, j):
+        rows = rows_at((y * 4 + slot_x) * OWN, OWN, OWN)
+        copy(txt.at[rows], txt.at[rows], TEXT2, plane_dev(x, lax.rem(y + j, 4))).start()
+
+    def send_own_y(j, _):
+        send_text_y(x, j)
+        return 0
+
+    lax.fori_loop(1, 4, send_own_y, 0)
 
     def text_on():
         got(txt.at[pl.ds(0, 3 * OWN)], TEXT)
-        rows = rows_at(y * 128, 128, 128)
-
-        def send(j, _):
-            copy(txt.at[rows], txt.at[rows], TEXT2, plane_dev(x, lax.rem(y + j, 4))).start()
+
+        def send(i, _):
+            send_text_y(lax.rem(x + 1 + i // 3, 4), 1 + lax.rem(i, 3))
             return 0
 
-        lax.fori_loop(1, 4, send, 0)
+        lax.fori_loop(0, 9, send, 0)
 
     def slot_of(f, way, far, flows):
         return pl.ds(((way * flows + f) * 4 + far - 1) * FLOW, FLOW)
@@ -292,6 +295,12 @@
     )
     forward(0)
     rs1_across((1, 0))
+    def send_text(j, _):
+        device = plane_dev(lax.rem(x + j, 4), y)
+        copy(txt.at[own_text], txt.at[own_text], TEXT, device).start()
+        return 0
+
+    lax.fori_loop(1, 4, send_text, 0)
     rs1_ring(4)
     forward(1)
     rs1_across((2, 3))
@@ -373,7 +382,6 @@
     low = weights - hi - mid
     hot[...] = jnp.concatenate([hi, mid, low, jnp.zeros((ext - 24, ROWS), F32)], axis=0).astype(BF16)
     meta[0:1, :] = meta[0:1, :] * 64.0 + meta[1:2, :]
-    got(txt.at[pl.ds(0, 3 * 128)], TEXT2)
 
     loss_acc[...] = jnp.zeros_like(loss_acc)
 
@@ -393,6 +401,21 @@
         slope = logit_scale * weight * (grown / (1.0 + grown))
         coef[:, images] = jnp.where(hit, -slope, slope).astype(BF16)
 
+    def image_grad(g):
+        rows = pl.ds(g * 128, 128)
+        ig[rows, :] = dot_tn(coef[:, rows], txt[:, :D])
+        to = pl.ds(g * 64, 64)
+        for slot in (2 * g, 2 * g + 1):
+            c_send[slot * OWN : slot * OWN + OWN, :] = ig[slot * 64 + OWN : slot * 64 + 64, :]
+        copy(c_send.at[to], c_recv.at[to], RS2C, partner, csem.at[5 + g]).start()
+
+    def both_cores(g):
+        to = pl.ds(g * 64, 64)
+        copy(c_send.at[to], c_recv.at[to], RS2C, partner, csem.at[5 + g]).wait_recv()
+        for slot in (2 * g, 2 * g + 1):
+            rows = pl.ds(slot * OWN, OWN)
+            held[rows, :] = ig[slot * 64 : slot * 64 + OWN, :] + c_recv[rows, :]
+
     for way in (UP, DOWN):
         got_img(OWN, 2 + way)
         to_partner(slot_at(1 - way, 1))
@@ -403,6 +426,7 @@
         send_img(row + FLOW * way, 64 + FLOW * way, FLOW, 6 + way, 2 * sign)
     for way in (UP, DOWN):
         to_partner(slot_at(1 - way, 2))
+    got(txt.at[pl.ds(0, 3 * 128)], TEXT2)
     from_partner(1)
     pairs(3)
     for way in (UP, DOWN):
@@ -410,29 +434,16 @@
         to_partner(slot_at(1 - way, 3))
     from_partner(2)
     pairs(2)
+    image_grad(3)
     for way in (UP, DOWN):
         got_img(FLOW, 6 + way)
     to_partner(1)
     from_partner(3)
     pairs(1)
+    image_grad(1)
     from_partner(0)
     from_partner(4)
     pairs(0)
-
-    def image_grad(g):
-        rows = pl.ds(g * 128, 128)
-        ig[rows, :] = dot_tn(coef[:, rows], txt[:, :D])
-        to = pl.ds(g * 64, 64)
-        for slot in (2 * g, 2 * g + 1):
-            c_send[slot * OWN : slot * OWN + OWN, :] = ig[slot * 64 + OWN : slot * 64 + 64, :]
-        copy(c_send.at[to], c_recv.at[to], RS2C, partner, csem.at[5 + g]).start()
-
-    def both_cores(g):
-        to = pl.ds(g * 64, 64)
-        copy(c_send.at[to], c_recv.at[to], RS2C, partner, csem.at[5 + g]).wait_recv()
-        for slot in (2 * g, 2 * g + 1):
-            rows = pl.ds(slot * OWN, OWN)
-            held[rows, :] = ig[slot * 64 : slot * 64 + OWN, :] + c_recv[rows, :]
 
     def send_rs2(value, sem, distance):
         rows = pl.ds(sem * OWN, value.shape[0])
@@ -449,17 +460,14 @@
         return held[row : row + OWN, :]
 
     image_grad(0)
-    image_grad(1)
+    both_cores(1)
+    send_rs2(held_at(UP, 3), 2, 1)
+    send_rs2(held_at(DOWN, 3), 3, -1)
     both_cores(0)
     far4 = held_at(UP, 4)
     send_rs2(far4[:FLOW], 0, 2)
     send_rs2(far4[FLOW:], 1, -2)
     image_grad(2)
-    both_cores(1)
-    send_rs2(held_at(UP, 3), 2, 1)
-    send_rs2(held_at(DOWN, 3), 3, -1)
-    image_grad(3)
-    both_cores(2)
     both_cores(3)
     send_rs2(held_at(UP, 1), 6, 1)
     send_rs2(held_at(DOWN, 1), 7, -1)
@@ -472,6 +480,7 @@
         return 0
 
     lax.fori_loop(1, 3, text_grad, 0)
+    both_cores(2)
     far2 = held_at(UP, 2) + got_rs2(2)
     send_rs2(jnp.concatenate([far2[:FLOW] + got_rs2(0, FLOW), far2[FLOW:]], axis=0), 4, 2)
     far2 = held_at(DOWN, 2) + got_rs2(3)
@@ -589,7 +598,8 @@
         copy(ars_so.at[rows_at(q * 16, 16, 16)], ars_ro.at[rows_at((j - 1) * 16, 16, 16)], ARS_O, device).start()
         return 0
 
-    lax.fori_loop(1, 8, send_ars_out, 0)
+    for peer in FAR_FIRST:
+        send_ars_out(peer, 0)
     w_in_half(own_cols, awi, F32)
     got(arc_ri, ARC_I)
     awi[...] += arc_ri[...].astype(F32)
@@ -600,7 +610,8 @@
         copy(ars_si.at[rows_at(q * 144, 144, 144)], ars_ri.at[rows_at((j - 1) * 144, 144, 144)], ARS_I, device).start()
         return 0
 
-    lax.fori_loop(1, 8, send_ars_in, 0)
+    for peer in FAR_FIRST:
+        send_ars_in(peer, 0)
     text_grad_on()
     rs3_ring(2)
     got(l1r, LOSS1)
@@ -625,7 +636,8 @@
         copy(fwo.at[core, own_out], fwo.at[core, own_out], AAG_O, device, aagsem.at[7 + j]).start()
         return 0
 
-    lax.fori_loop(1, 8, send_aag_out, 0)
+    for peer in FAR_FIRST:
+        send_aag_out(peer, 0)
     copy(fwo.at[core, own_out], fwo.at[core, own_out], AFC_O, partner).start()
     got(ars_ri, ARS_I)
     for j in range(7):
@@ -637,7 +649,8 @@
         copy(fwi.at[core, own_in], fwi.at[core, own_in], AAG_I, device, aagsem.at[j - 1]).start()
         return 0
 
-    lax.fori_loop(1, 8, send_aag_in, 0)
+    for peer in FAR_FIRST:
+        send_aag_in(peer, 0)
     copy(fwi.at[core, own_in], fwi.at[core, own_in], AFC_I, partner).start()
     got(lcr, LOSSC)
     lz_tile[...] = loss + lcr[...]
@@ -661,7 +674,8 @@
         copy(fwi.at[core, into], fwi.at[core, into], AFC_I, partner).start()
         return 0
 
-    lax.fori_loop(1, 8, weights_on, 0)
+    for peer in FAR_FIRST:
+        weights_on(peer, 0)
     got(tgr2, TG2)
     grad_text = tgo[rows_at(x * OWN, OWN, OWN), :]
     for j in range(3):
@@ -672,15 +686,6 @@
     for j in range(7):
         loss = loss + lzr[j * 8 : j * 8 + 8, :]
     loss_ref[...] = loss * (1.0 / PAIRS)
-
-    got(rs3xr, RS3X)
-    gi_ref[...] = grad_image + rs3xr[...]
-    got(fwo.at[1 - core], AFC_O)
-    for half in range(2):
-        gwo_ref[half * 128 : half * 128 + 128, :] = fwo[half]
-    got(fwi.at[1 - core], AFC_I)
-    for half in range(2):
-        gwi_ref[:, half * 128 : half * 128 + 128] = fwi[half]
 
     sent(txt.at[pl.ds(0, 3 * OWN)], TEXT)
     sent(txt.at[pl.ds(0, 3 * 128)], TEXT2)
@@ -694,16 +699,25 @@
     sent(c_send, RS2C)
     sent(rs2s.at[pl.ds(0, 14 * FLOW)], RS2Z)
     sent(tgr, TG)
-    sent(tgr2, TG2)
     sent(l1r, LOSS1)
     sent(lc_tile, LOSSC)
-    sent(lzr, LOSSZ)
     sent(gfall.at[pl.ds(0, 21 * FLOW)], AG2)
     sent(gfall.at[pl.ds(0, 9 * FLOW)], AG2X)
+    sent(arc_si, ARC_I)
+    sent(arc_so, ARC_O)
+    got(rs3xr, RS3X)
+    gi_ref[...] = grad_image + rs3xr[...]
+    got(fwo.at[1 - core], AFC_O)
+    for half in range(2):
+        gwo_ref[half * 128 : half * 128 + 128, :] = fwo[half]
+    got(fwi.at[1 - core], AFC_I)
+    for half in range(2):
+        gwi_ref[:, half * 128 : half * 128 + 128] = fwi[half]
+
+    sent(tgr2, TG2)
+    sent(lzr, LOSSZ)
     sent(rs3s.at[pl.ds(0, 28 * FLOW)], RS3)
     sent(rs3xs, RS3X)
-    sent(arc_si, ARC_I)
-    sent(arc_so, ARC_O)
     sent(ars_ri, ARS_I)
     sent(ars_ro, ARS_O)
     sent(fwi.at[0, pl.ds(0, 7 * 144)], AAG_I)

time: 107 us -> 107 us (level)
  no operation moved by 1% of the time
where the time goes in v6:
time: 107 us
  Pallas kernels  106 us (99%)
    pallas_call x1, Pallas kernels, per_device(): pl.pallas_call(kernel, out_shape=(jax.ShapeDtypeStruct((8, 128), F32), ja...  103 us
    pallas_call x1, Pallas kernels, per_device(): pl.pallas_call(widen, out_shape=(jax.ShapeDtypeStruct((1, 1), F32), jax.S...  2.9 us

profile of v6, /device:TPU:1, one launch (start us, length us, event | category | flops | bytes accessed | tf_op | source)
XLA Modules:
  0.0 106.7 jit_solution(13684189605723221286)
XLA Ops:
  0.6 103.1 %pairs_and_block.1 = (f32[8,128]{1,0:T(8,128)}, f32[32,1152]{1,0:T(8,128)}, f32[32,1152]{1,0:T(8,128)}, bf16[1152,256]{1,0:T(8,128)(2,1)}, bf16[256,1152]{1,0:T(8,128)(2,1)}) custom-call(bf16[512,1152]{1,0:T(8,128)(2,1)} %x_hbm.1, bf16[32,1152]{1,0:T(8,128)(2,1)} %t_hbm.1, bf16[1152,256]{1,0:T(8,128)(2,1)} %wi_hbm.1, bf16[256,1152]{1,0:T(8,128)(2,1)} %wo_hbm.1, ...), custom_call_target="tpu_custom_call" | custom-call | tf_op jit(solution)/shard_map/pairs_and_block/pallas_call | solution.py:824
  103.8 2.9 %widen.1 = (f32[1,1]{1,0:T(1,128)}, f32[32,1152]{1,0:T(8,128)}, f32[32,1152]{1,0:T(8,128)}, f32[1152,256]{1,0:T(8,128)}, f32[256,1152]{1,0:T(8,128)}) custom-call(f32[8,128]{1,0:T(8,128)} %get-tuple-element.15.loss_in, f32[32,1152]{1,0:T(8,128)} %get-tuple-element.16.gt_in, f32[32,1152]{1,0:T(8,128)} %get-tuple-element.17.gi_in, ...), custom_call_target="tpu_custom_call" | custom-call | tf_op jit(solution)/shard_map/widen/pallas_call | solution.py:844

commit v7 on v6

--- a/solution.py
+++ b/solution.py
@@ -585,9 +585,6 @@
     backward(0)
     w_in_half(other_cols, arc_si, BF16)
     copy(arc_si, arc_ri, ARC_I, partner).start()
-    to_input(0)
-    rs3_ring(4)
-    rs3_ring(3)
     awo[...] = swo[own_cols, :] + dot_tn(act[late, own_cols], gfall[late, :])
     got(arc_ro, ARC_O)
     awo[...] += arc_ro[...].astype(F32)
@@ -600,6 +597,9 @@
 
     for peer in FAR_FIRST:
         send_ars_out(peer, 0)
+    to_input(0)
+    rs3_ring(4)
+    rs3_ring(3)
     w_in_half(own_cols, awi, F32)
     got(arc_ri, ARC_I)
     awi[...] += arc_ri[...].astype(F32)

time: 107 us -> 110 us (1.028)
  Pallas kernels: 106 us -> 109 us
    pallas_call x1, Pallas kernels: 103 us -> 106 us  [per_device(): pl.pallas_call(kernel, out_shape=(jax.ShapeDtypeStruct((8, 128), F32), ja...]
where the time goes in v7:
time: 110 us
  Pallas kernels  109 us (99%)
    pallas_call x1, Pallas kernels, per_device(): pl.pallas_call(kernel, out_shape=(jax.ShapeDtypeStruct((8, 128), F32), ja...  106 us
    pallas_call x1, Pallas kernels, per_device(): pl.pallas_call(widen, out_shape=(jax.ShapeDtypeStruct((1, 1), F32), jax.S...  2.9 us

profile of v7, /device:TPU:1, one launch (start us, length us, event | category | flops | bytes accessed | tf_op | source)
XLA Modules:
  0.0 109.6 jit_solution(10113555978184334392)
XLA Ops:
  0.6 106.1 %pairs_and_block.1 = (f32[8,128]{1,0:T(8,128)}, f32[32,1152]{1,0:T(8,128)}, f32[32,1152]{1,0:T(8,128)}, bf16[1152,256]{1,0:T(8,128)(2,1)}, bf16[256,1152]{1,0:T(8,128)(2,1)}) custom-call(bf16[512,1152]{1,0:T(8,128)(2,1)} %x_hbm.1, bf16[32,1152]{1,0:T(8,128)(2,1)} %t_hbm.1, bf16[1152,256]{1,0:T(8,128)(2,1)} %wi_hbm.1, bf16[256,1152]{1,0:T(8,128)(2,1)} %wo_hbm.1, ...), custom_call_target="tpu_custom_call" | custom-call | tf_op jit(solution)/shard_map/pairs_and_block/pallas_call | solution.py:824
  106.7 2.9 %widen.1 = (f32[1,1]{1,0:T(1,128)}, f32[32,1152]{1,0:T(8,128)}, f32[32,1152]{1,0:T(8,128)}, f32[1152,256]{1,0:T(8,128)}, f32[256,1152]{1,0:T(8,128)}) custom-call(f32[8,128]{1,0:T(8,128)} %get-tuple-element.15.loss_in, f32[32,1152]{1,0:T(8,128)} %get-tuple-element.16.gt_in, f32[32,1152]{1,0:T(8,128)} %get-tuple-element.17.gi_in, ...), custom_call_target="tpu_custom_call" | custom-call | tf_op jit(solution)/shard_map/widen/pallas_call | solution.py:844
